TPU v7x, 128 devices: a whole 4x4x4 slice. The times are simulated.
128 devices in a mesh: row: 16 (over z_lo, y, core), col: 8 (over z_hi, x).
Axes of the slice: x: 4, y: 4, z: 4 (z_hi: 2, z_lo: 2; z = z_hi * 2 + z_lo), core: 2. Of those that a mesh axis runs over, the one named last changes fastest.
Arguments:
- hidden_in: float32 [16384, 1024], P('row', 'col'), may hold values from -6 to 6
- joined_weight: bfloat16 [2, 1024, 3072], P(None, 'row', 'col'), may hold values from -0.1875 to 0.1875
- query_bias: bfloat16 [2, 1024], P(None, ('col', 'row')), may hold values from -3 to 3
- value_bias: bfloat16 [2, 1024], P(None, ('col', 'row')), may hold values from -1.75 to 1.75
- out_weight: bfloat16 [2, 1024, 1024], P(None, 'col', 'row'), may hold values from -0.5 to 0.5
- out_bias: bfloat16 [2, 1024], P(None, ('col', 'row')), may hold values from -1.75 to 1.75
- first_gain: bfloat16 [2, 1024], P(None, ('col', 'row')), may hold values from 0.25 to 1.75
- first_shift: bfloat16 [2, 1024], P(None, ('col', 'row')), may hold values from -1.75 to 1.75
- up_weight: bfloat16 [2, 1024, 4096], P(None, 'row', 'col'), may hold values from -0.1875 to 0.1875
- up_bias: bfloat16 [2, 4096], P(None, ('col', 'row')), may hold values from -1.75 to 1.75
- down_weight: bfloat16 [2, 4096, 1024], P(None, 'col', 'row'), may hold values from -0.09375 to 0.09375
- down_bias: bfloat16 [2, 1024], P(None, ('col', 'row')), may hold values from -1.75 to 1.75
- second_gain: bfloat16 [2, 1024], P(None, ('col', 'row')), may hold values from 0.25 to 1.75
- second_shift: bfloat16 [2, 1024], P(None, ('col', 'row')), may hold values from -1.75 to 1.75
- seq_lengths: int32 [16, 4], P('row'), may hold values from 0 to 1024, as said below
- cotangent: float32 [16384, 1024], P('row', 'col'), may hold values from -6 to 6
Outputs:
- hidden_out: float32 [16384, 1024], P('row', 'col')
- grad_hidden: float32 [16384, 1024], P('row', 'col')
- grad_joined_weight: float32 [2, 1024, 3072], P(None, 'row', 'col')
- grad_query_bias: float32 [2, 1024], P(None, ('col', 'row'))
- grad_value_bias: float32 [2, 1024], P(None, ('col', 'row'))
- grad_out_weight: float32 [2, 1024, 1024], P(None, 'col', 'row')
- grad_out_bias: float32 [2, 1024], P(None, ('col', 'row'))
- grad_first_gain: float32 [2, 1024], P(None, ('col', 'row'))
- grad_first_shift: float32 [2, 1024], P(None, ('col', 'row'))
- grad_up_weight: float32 [2, 1024, 4096], P(None, 'row', 'col')
- grad_up_bias: float32 [2, 4096], P(None, ('col', 'row'))
- grad_down_weight: float32 [2, 4096, 1024], P(None, 'col', 'row')
- grad_down_bias: float32 [2, 1024], P(None, ('col', 'row'))
- grad_second_gain: float32 [2, 1024], P(None, ('col', 'row'))
- grad_second_shift: float32 [2, 1024], P(None, ('col', 'row'))
Inputs may be any that keep to these rules, and one draw needn't show every extreme that they name: `seq_lengths`: each group's 4 lengths sum to between 512 and 1024, the rest of its 1024 rows being padding; in one group, drawn from the seed, a single sequence fills all 1024 rows. Lengths may be 0.
All inputs are finite; a program needn't handle non-finite values.
Results may differ from a plain program's by a relative error of at most 0.04.
Values may be sent and summed in bfloat16 or wider, within the bound.
A program may use at most 128 MiB of HBM per device.

v0:
```python
import jax
import jax.numpy as jnp
from jax import lax
from jax.sharding import PartitionSpec as P

D = 1024
HEADS = 16
HDIM = 64


EPS = 1e-05
NEG = -1000000000.0


def gelu_tanh(values):
    return (
        0.5
        * values
        * (1.0 + jnp.tanh(0.7978845608028654 * (values + 0.044715 * values * values * values)))
    )


def feature_sums(first_sum, second_sum):
    return lax.psum((first_sum, second_sum), "col")


def gather_features(rounded):
    return lax.all_gather(rounded, "col", axis=1, tiled=True)


def gather_grads(rounded):
    return lax.all_gather(rounded, "col", axis=1, tiled=True)


def spread_sum(partial_rows):
    return lax.psum_scatter(
        partial_rows.astype(jnp.bfloat16), "col", scatter_dimension=1, tiled=True
    ).astype(jnp.float32)


def spread_grad(partial_rows):
    return lax.psum_scatter(
        partial_rows.astype(jnp.bfloat16), "col", scatter_dimension=1, tiled=True
    ).astype(jnp.float32)


def slice_layer(params, layer_index):
    (
        joined_weight,
        query_bias,
        value_bias,
        out_weight,
        out_bias,
        first_gain,
        first_shift,
        up_weight,
        up_bias,
        down_weight,
        down_bias,
        second_gain,
        second_shift,
    ) = params
    vectors = jnp.stack(
        [
            first_gain[layer_index],
            first_shift[layer_index],
            query_bias[layer_index],
            value_bias[layer_index],
            out_bias[layer_index],
            second_gain[layer_index],
            second_shift[layer_index],
            down_bias[layer_index],
        ]
    )
    return (
        joined_weight[layer_index],
        out_weight[layer_index],
        up_weight[layer_index],
        down_weight[layer_index],
        vectors,
        up_bias[layer_index],
    )


def fetch_layer(params, layer_index):
    joined_part, out_part, up_part, down_part, vectors, up_bias_part = slice_layer(
        params, layer_index
    )
    return (
        lax.all_gather(joined_part, "row", axis=0, tiled=True),
        lax.all_gather(out_part, "row", axis=1, tiled=True),
        lax.all_gather(up_part, "row", axis=0, tiled=True),
        lax.all_gather(down_part, "row", axis=1, tiled=True),
        lax.all_gather(vectors, "row", axis=1, tiled=True),
        lax.all_gather(up_bias_part, "row", axis=0, tiled=True),
    )


def fetch_again(params, layer_index):
    joined_part, out_part, up_part, down_part, vectors, up_bias_part = slice_layer(
        params, layer_index
    )
    return (
        lax.all_gather(joined_part, "row", axis=0, tiled=True),
        lax.all_gather(out_part, "row", axis=1, tiled=True),
        lax.all_gather(up_part, "row", axis=0, tiled=True),
        lax.all_gather(down_part, "row", axis=1, tiled=True),
        lax.all_gather(vectors, "row", axis=1, tiled=True),
        lax.all_gather(up_bias_part, "row", axis=0, tiled=True),
    )


def norm_forward(hidden, gain, shift):
    row_total, squares = feature_sums(jnp.sum(hidden, axis=1), jnp.sum(hidden * hidden, axis=1))
    mean_rows = row_total / D
    inverse = lax.rsqrt(squares / D - mean_rows * mean_rows + EPS)
    normed = (hidden - mean_rows[:, None]) * inverse[:, None]
    return (normed, inverse, (normed * gain + shift).astype(jnp.bfloat16))


def norm_backward(grad_rows, normed, inverse, gain):
    grad_gain = jnp.sum(grad_rows * normed, axis=0)
    grad_shift = jnp.sum(grad_rows, axis=0)
    scaled = grad_rows * gain
    row_total, paired = feature_sums(jnp.sum(scaled, axis=1), jnp.sum(scaled * normed, axis=1))
    grad_input = inverse[:, None] * (scaled - row_total[:, None] / D - normed * paired[:, None] / D)
    return (grad_input, grad_gain, grad_shift)


def block_scores(query_block, key_rows, first_row, segment, slopes, score_scale):
    block_rows = query_block.shape[0]
    row_index = first_row + jnp.arange(block_rows, dtype=jnp.int32)
    columns = jnp.arange(key_rows.shape[0], dtype=jnp.int32)
    offset = (columns[None, :] - row_index[:, None]).astype(jnp.float32)
    scores = (
        jnp.einsum("qhd,khd->hqk", query_block, key_rows, preferred_element_type=jnp.float32)
        * score_scale
    )
    scores = scores + slopes[:, None, None] * offset[None]
    row_segment = lax.dynamic_slice_in_dim(segment, first_row, block_rows)
    allowed = (row_segment[:, None] == segment[None, :]) & (columns[None, :] <= row_index[:, None])
    return jnp.where(allowed[None], scores, NEG)


def attend_forward(query_rows, key_rows, value_rows, segment, slopes, score_scale, block_rows):
    block_count = query_rows.shape[0] // block_rows

    def one_block(block_index):
        first_row = block_index * block_rows
        query_block = lax.dynamic_slice_in_dim(query_rows, first_row, block_rows)
        scores = block_scores(query_block, key_rows, first_row, segment, slopes, score_scale)
        row_max = jnp.max(scores, axis=-1, keepdims=True)
        shifted = jnp.exp(scores - row_max)
        row_total = jnp.sum(shifted, axis=-1, keepdims=True)
        soft_probs = (shifted / row_total).astype(jnp.bfloat16)
        mixed_block = jnp.einsum(
            "hqk,khd->qhd", soft_probs, value_rows, preferred_element_type=jnp.float32
        )
        return (mixed_block.astype(jnp.bfloat16), (row_max + jnp.log(row_total))[..., 0])

    mixed_heads, log_totals = lax.map(one_block, jnp.arange(block_count, dtype=jnp.int32))
    return (mixed_heads.reshape(query_rows.shape), log_totals)


def attend_backward(
    query_rows,
    key_rows,
    value_rows,
    grad_heads,
    log_totals,
    segment,
    slopes,
    score_scale,
    block_rows,
):
    block_count = query_rows.shape[0] // block_rows

    def one_block(carried, block_index):
        grad_keys, grad_values = carried
        first_row = block_index * block_rows
        query_block = lax.dynamic_slice_in_dim(query_rows, first_row, block_rows)
        grad_block = lax.dynamic_slice_in_dim(grad_heads, first_row, block_rows)
        scores = block_scores(query_block, key_rows, first_row, segment, slopes, score_scale)
        soft_probs = jnp.exp(scores - log_totals[block_index][..., None])
        grad_probs = jnp.einsum(
            "qhd,khd->hqk", grad_block, value_rows, preferred_element_type=jnp.float32
        )
        inner_sum = jnp.sum(soft_probs * grad_probs, axis=-1, keepdims=True)
        grad_scores = (soft_probs * (grad_probs - inner_sum)).astype(jnp.bfloat16)
        grad_query = (
            jnp.einsum("hqk,khd->qhd", grad_scores, key_rows, preferred_element_type=jnp.float32)
            * score_scale
        )
        grad_keys = (
            grad_keys
            + jnp.einsum(
                "hqk,qhd->khd", grad_scores, query_block, preferred_element_type=jnp.float32
            )
            * score_scale
        )
        grad_values = grad_values + jnp.einsum(
            "hqk,qhd->khd",
            soft_probs.astype(jnp.bfloat16),
            grad_block,
            preferred_element_type=jnp.float32,
        )
        return ((grad_keys, grad_values), grad_query)

    zero_rows = jnp.zeros(key_rows.shape, jnp.float32)
    (grad_keys, grad_values), grad_queries = lax.scan(
        one_block, (zero_rows, zero_rows), jnp.arange(block_count, dtype=jnp.int32)
    )
    return (grad_queries.reshape(query_rows.shape), grad_keys, grad_values)


def layer_forward(hidden, pieces, segment, head_start):
    joined_full, out_full, up_full, down_full, vector_rows, up_bias_rows = pieces
    vectors = vector_rows.astype(jnp.float32)
    token_count = hidden.shape[0]
    normed_one, inverse_one, first_rows = norm_forward(hidden, vectors[0], vectors[1])
    first_full = gather_features(first_rows)
    local_heads = joined_full.shape[1] // (3 * HDIM)
    joined_rows = jnp.dot(first_full, joined_full, preferred_element_type=jnp.float32).reshape(
        token_count, local_heads, 3, HDIM
    )
    query_rows = (joined_rows[:, :, 0] + vectors[2].reshape(local_heads, HDIM)).astype(jnp.bfloat16)
    key_rows = joined_rows[:, :, 1].astype(jnp.bfloat16)
    value_rows = (joined_rows[:, :, 2] + vectors[3].reshape(local_heads, HDIM)).astype(jnp.bfloat16)
    head_numbers = (head_start * local_heads + jnp.arange(local_heads, dtype=jnp.int32)).astype(
        jnp.float32
    )
    slopes = jnp.exp2(-8.0 * (head_numbers + 1.0) / HEADS)
    block_rows = min(512, token_count)
    mixed_heads, log_totals = attend_forward(
        query_rows, key_rows, value_rows, segment, slopes, HDIM ** (-0.5), block_rows
    )
    heads_flat = mixed_heads.reshape(token_count, -1)
    branch = (
        spread_sum(jnp.dot(heads_flat, out_full, preferred_element_type=jnp.float32)) + vectors[4]
    )
    middle = hidden + branch
    normed_two, inverse_two, second_rows = norm_forward(middle, vectors[5], vectors[6])
    second_full = gather_features(second_rows)
    up_rows = jnp.dot(
        second_full, up_full, preferred_element_type=jnp.float32
    ) + up_bias_rows.astype(jnp.float32)
    activated = gelu_tanh(up_rows).astype(jnp.bfloat16)
    down_rows = (
        spread_sum(jnp.dot(activated, down_full, preferred_element_type=jnp.float32)) + vectors[7]
    )
    saved_rows = (
        normed_one,
        inverse_one,
        first_full,
        query_rows,
        key_rows,
        value_rows,
        log_totals,
        heads_flat,
        normed_two,
        inverse_two,
        second_full,
        up_rows,
        activated,
        slopes,
    )
    return (middle + down_rows, saved_rows)


def layer_backward(grad_next, pieces, saved_rows, segment):
    joined_full, out_full, up_full, down_full, vector_rows, up_bias_rows = pieces
    vectors = vector_rows.astype(jnp.float32)
    (
        normed_one,
        inverse_one,
        first_full,
        query_rows,
        key_rows,
        value_rows,
        log_totals,
        heads_flat,
        normed_two,
        inverse_two,
        second_full,
        up_rows,
        activated,
        slopes,
    ) = saved_rows
    token_count = grad_next.shape[0]
    grad_down = grad_next.astype(jnp.bfloat16)
    down_bias_grad = jnp.sum(grad_down.astype(jnp.float32), axis=0)
    grad_down_full = gather_grads(grad_down)
    grad_act = jnp.dot(grad_down_full, down_full.T, preferred_element_type=jnp.float32)
    down_weight_grad = jnp.dot(activated.T, grad_down_full, preferred_element_type=jnp.float32)
    _, gelu_pull = jax.vjp(gelu_tanh, up_rows)
    grad_up = gelu_pull(grad_act)[0].astype(jnp.bfloat16)
    up_bias_grad = jnp.sum(grad_up.astype(jnp.float32), axis=0)
    up_weight_grad = jnp.dot(second_full.T, grad_up, preferred_element_type=jnp.float32)
    grad_second = spread_grad(jnp.dot(grad_up, up_full.T, preferred_element_type=jnp.float32))
    grad_norm_two, second_gain_grad, second_shift_grad = norm_backward(
        grad_second, normed_two, inverse_two, vectors[5]
    )
    grad_middle = grad_next + grad_norm_two
    grad_branch = grad_middle.astype(jnp.bfloat16)
    out_bias_grad = jnp.sum(grad_branch.astype(jnp.float32), axis=0)
    grad_branch_full = gather_grads(grad_branch)
    out_weight_grad = jnp.dot(heads_flat.T, grad_branch_full, preferred_element_type=jnp.float32)
    grad_heads = jnp.dot(grad_branch_full, out_full.T, preferred_element_type=jnp.float32).astype(
        jnp.bfloat16
    )
    grad_heads = grad_heads.reshape(query_rows.shape)
    block_rows = min(512, token_count)
    grad_query, grad_keys, grad_values = attend_backward(
        query_rows,
        key_rows,
        value_rows,
        grad_heads,
        log_totals,
        segment,
        slopes,
        HDIM ** (-0.5),
        block_rows,
    )
    query_low = grad_query.astype(jnp.bfloat16)
    key_low = grad_keys.astype(jnp.bfloat16)
    value_low = grad_values.astype(jnp.bfloat16)
    query_bias_grad = jnp.sum(query_low.astype(jnp.float32), axis=0).reshape(-1)
    value_bias_grad = jnp.sum(value_low.astype(jnp.float32), axis=0).reshape(-1)
    grad_joined = jnp.stack([query_low, key_low, value_low], axis=2).reshape(token_count, -1)
    joined_weight_grad = jnp.dot(first_full.T, grad_joined, preferred_element_type=jnp.float32)
    grad_first = spread_grad(
        jnp.dot(grad_joined, joined_full.T, preferred_element_type=jnp.float32)
    )
    grad_norm_one, first_gain_grad, first_shift_grad = norm_backward(
        grad_first, normed_one, inverse_one, vectors[0]
    )
    grad_hidden = grad_middle + grad_norm_one
    vector_grads = jnp.stack(
        [
            first_gain_grad,
            first_shift_grad,
            query_bias_grad,
            value_bias_grad,
            out_bias_grad,
            second_gain_grad,
            second_shift_grad,
            down_bias_grad,
        ]
    )
    summed = (
        lax.psum_scatter(
            joined_weight_grad.astype(jnp.bfloat16), "row", scatter_dimension=0, tiled=True
        ).astype(jnp.float32),
        lax.psum_scatter(
            out_weight_grad.astype(jnp.bfloat16), "row", scatter_dimension=1, tiled=True
        ).astype(jnp.float32),
        lax.psum_scatter(
            up_weight_grad.astype(jnp.bfloat16), "row", scatter_dimension=0, tiled=True
        ).astype(jnp.float32),
        lax.psum_scatter(
            down_weight_grad.astype(jnp.bfloat16), "row", scatter_dimension=1, tiled=True
        ).astype(jnp.float32),
        lax.psum_scatter(
            vector_grads.astype(jnp.bfloat16), "row", scatter_dimension=1, tiled=True
        ).astype(jnp.float32),
        lax.psum_scatter(
            up_bias_grad.astype(jnp.bfloat16), "row", scatter_dimension=0, tiled=True
        ).astype(jnp.float32),
    )
    return (grad_hidden, summed)


def shards(
    hidden_in,
    joined_weight,
    query_bias,
    value_bias,
    out_weight,
    out_bias,
    first_gain,
    first_shift,
    up_weight,
    up_bias,
    down_weight,
    down_bias,
    second_gain,
    second_shift,
    seq_lengths,
    cotangent,
):
    params = (
        joined_weight,
        query_bias,
        value_bias,
        out_weight,
        out_bias,
        first_gain,
        first_shift,
        up_weight,
        up_bias,
        down_weight,
        down_bias,
        second_gain,
        second_shift,
    )
    token_count = hidden_in.shape[0]
    seq_ends = jnp.cumsum(seq_lengths[0])
    positions = jnp.arange(token_count, dtype=jnp.int32)
    segment = jnp.sum((positions[:, None] >= seq_ends[None, :]).astype(jnp.int32), axis=1)
    head_start = lax.axis_index("col")
    layers = joined_weight.shape[0]
    hidden = hidden_in
    kept_pieces = []
    kept_rows = []
    for layer_index in range(layers):
        pieces = fetch_layer(params, layer_index)
        hidden, saved_rows = layer_forward(hidden, pieces, segment, head_start)
        kept_pieces.append(pieces)
        kept_rows.append(saved_rows)
    grad_hidden = cotangent
    collected = []
    for layer_index in range(layers - 1, -1, -1):
        pieces = fetch_again(params, layer_index)
        grad_hidden, summed = layer_backward(grad_hidden, pieces, kept_rows[layer_index], segment)
        collected.insert(0, summed)
    stacked = [jnp.stack([layer_grads[member] for layer_grads in collected]) for member in range(6)]
    vector_grads = stacked[4]
    return (
        hidden,
        grad_hidden,
        stacked[0],
        vector_grads[:, 2],
        vector_grads[:, 3],
        stacked[1],
        vector_grads[:, 4],
        vector_grads[:, 0],
        vector_grads[:, 1],
        stacked[2],
        stacked[5],
        stacked[3],
        vector_grads[:, 7],
        vector_grads[:, 5],
        vector_grads[:, 6],
    )


def solution(mesh):
    return jax.shard_map(
        shards,
        mesh=mesh,
        in_specs=(
            P("row", "col"),
            P(None, "row", "col"),
            P(None, ("col", "row")),
            P(None, ("col", "row")),
            P(None, "col", "row"),
            P(None, ("col", "row")),
            P(None, ("col", "row")),
            P(None, ("col", "row")),
            P(None, "row", "col"),
            P(None, ("col", "row")),
            P(None, "col", "row"),
            P(None, ("col", "row")),
            P(None, ("col", "row")),
            P(None, ("col", "row")),
            P("row", None),
            P("row", "col"),
        ),
        out_specs=(
            P("row", "col"),
            P("row", "col"),
            P(None, "row", "col"),
            P(None, ("col", "row")),
            P(None, ("col", "row")),
            P(None, "col", "row"),
            P(None, ("col", "row")),
            P(None, ("col", "row")),
            P(None, ("col", "row")),
            P(None, "row", "col"),
            P(None, ("col", "row")),
            P(None, "col", "row"),
            P(None, ("col", "row")),
            P(None, ("col", "row")),
            P(None, ("col", "row")),
        ),
        check_vma=False,
    )
```

profile of v0, /device:TPU:0, one launch (start us, length us, event | category | flops | bytes accessed | tf_op | source)
XLA Modules:
  0.0 1941.4 jit_solution(17660570518183311884)
XLA Ops:
  37.1 25.0 %all-reduce.13 = (f32[1024]{0:T(1024)S(1)}, f32[1024]{0:T(1024)S(1)}) all-reduce(f32[1024]{0:T(1024)S(1)} %get-tuple-element.390, f32[1024]{0:T(1024)S(1)} %get-tuple-element.389), channel_id=1, replica_groups=mesh['row'=16,'col'=8] {'col'}, use_global_device_ids=true, to_apply=%region_3.4 | all-reduce | flops 2048 | bytes 16384 | tf_op jit(solution)/shard_map/psum | solution.py:24
  140.3 72.2 %reduce-scatter.51.cloned.1.call-done = bf16[128,1024]{1,0:T(8,128)(2,1)} async-done(((bf16[1024,1024]{1,0:T(8,128)(2,1)}), bf16[128,1024]{1,0:T(8,128)(2,1)}) %reduce-scatter.51.cloned.1.call-update) | async-done | bytes 262160
  214.0 21.2 %all-reduce.12 = (f32[1024]{0:T(1024)S(1)}, f32[1024]{0:T(1024)S(1)}) all-reduce(f32[1024]{0:T(1024)S(1)} %get-tuple-element.388, f32[1024]{0:T(1024)S(1)} %get-tuple-element.387), channel_id=1, replica_groups=mesh['row'=16,'col'=8] {'col'}, use_global_device_ids=true, to_apply=%region_14.15 | all-reduce | flops 2048 | bytes 16384 | tf_op jit(solution)/shard_map/psum | solution.py:24
  238.9 27.5 %all-reduce.15 = (bf16[512]{0:T(512)(128)(2,1)S(1)}, bf16[512]{0:T(512)(128)(2,1)S(1)}) all-reduce(bf16[512]{0:T(512)(128)(2,1)S(1)} %dynamic-update-slice, bf16[512]{0:T(512)(128)(2,1)S(1)} %dynamic-update-slice.1), channel_id=5, replica_groups=mesh['row'=16,'col'=8] {'row'}, use_global_device_ids=true, to_apply=%add | all-reduce | flops 1024 | bytes 4096
  266.4 26.2 %all-gather.25.cloned.1.call-done = bf16[1024,1024]{1,0:T(8,128)(2,1)} async-done(((bf16[1024,128]{1,0:T(8,128)(2,1)}), bf16[1024,1024]{1,0:T(8,128)(2,1)}) %all-gather.25.cloned.1.call-update) | async-done | bytes 2097168 | tf_op jit(solution)/shard_map/all_gather | solution.py:28
  297.1 29.1 %all-gather.41.cloned.1.call-done = bf16[1,512,1024]{1,2,0:T(8,128)(2,1)} async-done(((bf16[1,512,64]{1,2,0:T(8,128)(2,1)}), bf16[1,512,1024]{1,2,0:T(8,128)(2,1)}) %all-gather.41.cloned.1.call-update) | async-done | bytes 1048592 | tf_op jit(solution)/shard_map/all_gather | solution.py:93
  351.5 56.5 %reduce-scatter.53.cloned.1.call-done = bf16[128,1024]{1,0:T(8,128)(2,1)} async-done(((bf16[1024,1024]{1,0:T(8,128)(2,1)}), bf16[128,1024]{1,0:T(8,128)(2,1)}) %reduce-scatter.53.cloned.1.call-update) | async-done | bytes 262160
  409.5 21.3 %all-reduce.11 = (f32[1024]{0:T(1024)S(1)}, f32[1024]{0:T(1024)S(1)}) all-reduce(f32[1024]{0:T(1024)S(1)} %get-tuple-element.386, f32[1024]{0:T(1024)S(1)} %get-tuple-element.385), channel_id=1, replica_groups=mesh['row'=16,'col'=8] {'col'}, use_global_device_ids=true, to_apply=%region_19.20 | all-reduce | flops 2048 | bytes 16384 | tf_op jit(solution)/shard_map/psum | solution.py:24
  513.7 73.0 %reduce-scatter.55.cloned.1.call-done = bf16[128,1024]{1,0:T(8,128)(2,1)} async-done(((bf16[1024,1024]{1,0:T(8,128)(2,1)}), bf16[128,1024]{1,0:T(8,128)(2,1)}) %reduce-scatter.55.cloned.1.call-update) | async-done | bytes 262160
  588.1 21.2 %all-reduce.10 = (f32[1024]{0:T(1024)S(1)}, f32[1024]{0:T(1024)S(1)}) all-reduce(f32[1024]{0:T(1024)S(1)} %get-tuple-element.384, f32[1024]{0:T(1024)S(1)} %get-tuple-element.383), channel_id=1, replica_groups=mesh['row'=16,'col'=8] {'col'}, use_global_device_ids=true, to_apply=%region_28.29 | all-reduce | flops 2048 | bytes 16384 | tf_op jit(solution)/shard_map/psum | solution.py:24
  612.9 53.8 %all-gather.29.cloned.1.call-done = bf16[1024,1024]{1,0:T(8,128)(2,1)} async-done(((bf16[1024,128]{1,0:T(8,128)(2,1)}), bf16[1024,1024]{1,0:T(8,128)(2,1)}) %all-gather.29.cloned.1.call-update) | async-done | bytes 2097168 | tf_op jit(solution)/shard_map/all_gather | solution.py:28
  671.2 29.1 %all-gather.45.cloned.1.call-done = bf16[1,512,1024]{1,2,0:T(8,128)(2,1)} async-done(((bf16[1,512,64]{1,2,0:T(8,128)(2,1)}), bf16[1,512,1024]{1,2,0:T(8,128)(2,1)}) %all-gather.45.cloned.1.call-update) | async-done | bytes 1048592 | tf_op jit(solution)/shard_map/all_gather | solution.py:93
  709.0 52.4 %all-gather.31.cloned.1.call-done = bf16[1024,1024]{1,0:T(8,128)(2,1)} async-done(((bf16[1024,128]{1,0:T(8,128)(2,1)}), bf16[1024,1024]{1,0:T(8,128)(2,1)}) %all-gather.31.cloned.1.call-update) | async-done | bytes 2097168 | tf_op jit(solution)/shard_map/all_gather | solution.py:32
  792.0 76.4 %reduce-scatter.59.cloned.1.call-done = bf16[128,1024]{1,0:T(8,128)(2,1)} async-done(((bf16[1024,1024]{1,0:T(8,128)(2,1)}), bf16[128,1024]{1,0:T(8,128)(2,1)}) %reduce-scatter.59.cloned.1.call-update) | async-done | bytes 262160
  871.1 21.2 %all-reduce.9 = (f32[1024]{0:T(1024)S(1)}, f32[1024]{0:T(1024)S(1)}) all-reduce(f32[1024]{0:T(1024)S(1)} %get-tuple-element.380, f32[1024]{0:T(1024)S(1)} %get-tuple-element.392), channel_id=1, replica_groups=mesh['row'=16,'col'=8] {'col'}, use_global_device_ids=true, to_apply=%region_34.35 | all-reduce | flops 2048 | bytes 16384 | tf_op jit(solution)/shard_map/psum | solution.py:24
  894.8 56.0 %all-gather.33.cloned.1.call-done = bf16[1024,1024]{1,0:T(8,128)(2,1)} async-done(((bf16[1024,128]{1,0:T(8,128)(2,1)}), bf16[1024,1024]{1,0:T(8,128)(2,1)}) %all-gather.33.cloned.1.call-update) | async-done | bytes 2097168 | tf_op jit(solution)/shard_map/all_gather | solution.py:32
  980.1 74.2 %reduce-scatter.61.cloned.1.call-done = bf16[128,1024]{1,0:T(8,128)(2,1)} async-done(((bf16[1024,1024]{1,0:T(8,128)(2,1)}), bf16[128,1024]{1,0:T(8,128)(2,1)}) %reduce-scatter.61.cloned.1.call-update) | async-done | bytes 262160
  1056.1 21.3 %all-reduce.8 = (f32[1024]{0:T(1024)S(1)}, f32[1024]{0:T(1024)S(1)}) all-reduce(f32[1024]{0:T(1024)S(1)} %get-tuple-element.382, f32[1024]{0:T(1024)S(1)} %get-tuple-element.391), channel_id=1, replica_groups=mesh['row'=16,'col'=8] {'col'}, use_global_device_ids=true, to_apply=%region_42.43 | all-reduce | flops 2048 | bytes 16384 | tf_op jit(solution)/shard_map/psum | solution.py:24
  1079.3 56.0 %all-gather.35.cloned.1.call-done = bf16[1024,1024]{1,0:T(8,128)(2,1)} async-done(((bf16[1024,128]{1,0:T(8,128)(2,1)}), bf16[1024,1024]{1,0:T(8,128)(2,1)}) %all-gather.35.cloned.1.call-update) | async-done | bytes 2097168 | tf_op jit(solution)/shard_map/all_gather | solution.py:32
  1146.5 74.3 %reduce-scatter.63.cloned.1.call-done = bf16[128,1024]{1,0:T(8,128)(2,1)} async-done(((bf16[1024,1024]{1,0:T(8,128)(2,1)}), bf16[128,1024]{1,0:T(8,128)(2,1)}) %reduce-scatter.63.cloned.1.call-update) | async-done | bytes 262160
  1222.6 21.2 %all-reduce.7 = (f32[1024]{0:T(1024)S(1)}, f32[1024]{0:T(1024)S(1)}) all-reduce(f32[1024]{0:T(1024)S(1)} %get-tuple-element.376, f32[1024]{0:T(1024)S(1)} %get-tuple-element.394), channel_id=1, replica_groups=mesh['row'=16,'col'=8] {'col'}, use_global_device_ids=true, to_apply=%region_47.48 | all-reduce | flops 2048 | bytes 16384 | tf_op jit(solution)/shard_map/psum | solution.py:24
  1265.1 36.7 %all-gather.37.cloned.1.call-done = bf16[1024,1024]{1,0:T(8,128)(2,1)} async-done(((bf16[1024,128]{1,0:T(8,128)(2,1)}), bf16[1024,1024]{1,0:T(8,128)(2,1)}) %all-gather.37.cloned.1.call-update) | async-done | bytes 2097168 | tf_op jit(solution)/shard_map/all_gather | solution.py:32
  1364.5 62.2 %reduce-scatter.47.cloned.1.call-done = bf16[512,64]{0,1:T(8,128)(2,1)} async-done(((bf16[512,1024]{0,1:T(8,128)(2,1)}), bf16[512,64]{0,1:T(8,128)(2,1)}) %reduce-scatter.47.cloned.1.call-update) | async-done | bytes 65552 | tf_op jit(solution)/shard_map/reduce_scatter | solution.py:360
  1428.3 60.9 %reduce-scatter.45.cloned.1.call-done = bf16[64,512]{1,0:T(8,128)(2,1)} async-done(((bf16[1024,512]{1,0:T(8,128)(2,1)}), bf16[64,512]{1,0:T(8,128)(2,1)}) %reduce-scatter.45.cloned.1.call-update) | async-done | bytes 65552 | tf_op jit(solution)/shard_map/reduce_scatter | solution.py:357
  1489.2 62.4 %reduce-scatter.43.cloned.1.call-done = bf16[64,512]{1,0:T(8,128)(2,1)} async-done(((bf16[1024,512]{1,0:T(8,128)(2,1)}), bf16[64,512]{1,0:T(8,128)(2,1)}) %reduce-scatter.43.cloned.1.call-update) | async-done | bytes 65552 | tf_op jit(solution)/shard_map/reduce_scatter | solution.py:357
  1553.7 58.8 %reduce-scatter.41.cloned.1.call-done = bf16[128,64]{0,1:T(8,128)(2,1)} async-done(((bf16[128,1024]{0,1:T(8,128)(2,1)}), bf16[128,64]{0,1:T(8,128)(2,1)}) %reduce-scatter.41.cloned.1.call-update) | async-done | bytes 16400 | tf_op jit(solution)/shard_map/reduce_scatter | solution.py:354
  1612.6 61.1 %reduce-scatter.39.cloned.1.call-done = bf16[128,64]{0,1:T(8,128)(2,1)} async-done(((bf16[128,1024]{0,1:T(8,128)(2,1)}), bf16[128,64]{0,1:T(8,128)(2,1)}) %reduce-scatter.39.cloned.1.call-update) | async-done | bytes 16400 | tf_op jit(solution)/shard_map/reduce_scatter | solution.py:354
  1675.1 60.8 %reduce-scatter.37.cloned.1.call-done = bf16[64,384]{1,0:T(8,128)(2,1)} async-done(((bf16[1024,384]{1,0:T(8,128)(2,1)}), bf16[64,384]{1,0:T(8,128)(2,1)}) %reduce-scatter.37.cloned.1.call-update) | async-done | bytes 49168 | tf_op jit(solution)/shard_map/reduce_scatter | solution.py:351
  1735.8 61.8 %reduce-scatter.35.cloned.1.call-done = bf16[64,384]{1,0:T(8,128)(2,1)} async-done(((bf16[1024,384]{1,0:T(8,128)(2,1)}), bf16[64,384]{1,0:T(8,128)(2,1)}) %reduce-scatter.35.cloned.1.call-update) | async-done | bytes 49168 | tf_op jit(solution)/shard_map/reduce_scatter | solution.py:351
  1799.2 77.3 %reduce-scatter.65.cloned.1.call-done = bf16[128,1024]{1,0:T(8,128)(2,1)} async-done(((bf16[1024,1024]{1,0:T(8,128)(2,1)}), bf16[128,1024]{1,0:T(8,128)(2,1)}) %reduce-scatter.65.cloned.1.call-update) | async-done | bytes 262160
  1879.4 28.3 %all-reduce.14 = (bf16[8,128]{1,0:T(8,128)(2,1)S(1)}, bf16[8,128]{1,0:T(8,128)(2,1)S(1)}, bf16[512]{0:T(512)(128)(2,1)S(1)}, bf16[512]{0:T(512)(128)(2,1)S(1)}) all-reduce(bf16[8,128]{1,0:T(8,128)(2,1)S(1)} %stack.194, bf16[8,128]{1,0:T(8,128)(2,1)S(1)} %stack.186, ...), channel_id=23, replica_groups=mesh['row'=16,'col'=8] {'row'}, use_global_device_ids=true, to_apply=%region_75.76.clone | all-reduce | flops 3072 | bytes 12288
  1908.6 22.9 %all-reduce.6 = (f32[1024]{0:T(1024)S(1)}, f32[1024]{0:T(1024)S(1)}) all-reduce(f32[1024]{0:T(1024)S(1)} %get-tuple-element.378, f32[1024]{0:T(1024)S(1)} %get-tuple-element.393), channel_id=1, replica_groups=mesh['row'=16,'col'=8] {'col'}, use_global_device_ids=true, to_apply=%region_55.56 | all-reduce | flops 2048 | bytes 16384 | tf_op jit(solution)/shard_map/psum | solution.py:24
  (457 shorter events, 471.6 us)
Async XLA Ops:
  8.0 108.4 %all-gather.23.cloned.1.call-start = ((), (), s32[]{:S(2)}) async-start(), calls=%async_computation.16 | async-start | bytes 2359296 | tf_op jit(solution)/shard_map/all_gather | solution.py:28
  64.8 147.7 %reduce-scatter.51.cloned.1.call-start = ((), (), s32[]{:S(2)}) async-start(), calls=%async_computation.36 | async-start | bytes 2359296
  138.7 127.6 %all-gather.39.cloned.1.call-start = ((), (), s32[]{:S(2)}) async-start(), calls=%async_computation.32 | async-start | bytes 1114112 | tf_op jit(solution)/shard_map/all_gather | solution.py:92
  140.3 152.3 %all-gather.25.cloned.1.call-start = ((), (), s32[]{:S(2)}) async-start(), calls=%async_computation.17 | async-start | bytes 2359296 | tf_op jit(solution)/shard_map/all_gather | solution.py:28
  236.3 89.8 %all-gather.41.cloned.1.call-start = ((), (), s32[]{:S(2)}) async-start(), calls=%async_computation.33 | async-start | bytes 1114112 | tf_op jit(solution)/shard_map/all_gather | solution.py:93
  237.1 171.0 %reduce-scatter.53.cloned.1.call-start = ((), (), s32[]{:S(2)}) async-start(), calls=%async_computation.37 | async-start | bytes 2359296
  332.1 157.0 %all-gather.27.cloned.1.call-start = ((), (), s32[]{:S(2)}) async-start(), calls=%async_computation.18 | async-start | bytes 2359296 | tf_op jit(solution)/shard_map/all_gather | solution.py:28
  431.9 154.8 %reduce-scatter.55.cloned.1.call-start = ((), (), s32[]{:S(2)}) async-start(), calls=%async_computation.38 | async-start | bytes 2359296
  512.8 100.1 %all-gather.43.cloned.1.call-start = ((), (), s32[]{:S(2)}) async-start(), calls=%async_computation.34 | async-start | bytes 1114112 | tf_op jit(solution)/shard_map/all_gather | solution.py:92
  513.6 153.1 %all-gather.29.cloned.1.call-start = ((), (), s32[]{:S(2)}) async-start(), calls=%async_computation.19 | async-start | bytes 2359296 | tf_op jit(solution)/shard_map/all_gather | solution.py:28
  610.5 89.8 %all-gather.45.cloned.1.call-start = ((), (), s32[]{:S(2)}) async-start(), calls=%async_computation.35 | async-start | bytes 1114112 | tf_op jit(solution)/shard_map/all_gather | solution.py:93
  611.1 150.3 %all-gather.31.cloned.1.call-start = ((), (), s32[]{:S(2)}) async-start(), calls=%async_computation.20 | async-start | bytes 2359296 | tf_op jit(solution)/shard_map/all_gather | solution.py:32
  612.4 178.4 %reduce-scatter.57.cloned.1.call-start = ((), (), s32[]{:S(2)}) async-start(), calls=%async_computation.39 | async-start | bytes 2359296
  708.9 159.5 %reduce-scatter.59.cloned.1.call-start = ((), (), s32[]{:S(2)}) async-start(), calls=%async_computation.40 | async-start | bytes 2359296
  775.0 175.8 %all-gather.33.cloned.1.call-start = ((), (), s32[]{:S(2)}) async-start(), calls=%async_computation.21 | async-start | bytes 2359296 | tf_op jit(solution)/shard_map/all_gather | solution.py:32
  894.5 159.8 %reduce-scatter.61.cloned.1.call-start = ((), (), s32[]{:S(2)}) async-start(), calls=%async_computation.41 | async-start | bytes 2359296
  980.0 155.2 %all-gather.35.cloned.1.call-start = ((), (), s32[]{:S(2)}) async-start(), calls=%async_computation.22 | async-start | bytes 2359296 | tf_op jit(solution)/shard_map/all_gather | solution.py:32
  1079.0 141.8 %reduce-scatter.63.cloned.1.call-start = ((), (), s32[]{:S(2)}) async-start(), calls=%async_computation.42 | async-start | bytes 2359296
  1146.4 155.3 %all-gather.37.cloned.1.call-start = ((), (), s32[]{:S(2)}) async-start(), calls=%async_computation.23 | async-start | bytes 2359296 | tf_op jit(solution)/shard_map/all_gather | solution.py:32
  1245.5 119.0 %reduce-scatter.49.cloned.1.call-start = ((), (), s32[]{:S(2)}) async-start(), calls=%async_computation.31 | async-start | bytes 1114112 | tf_op jit(solution)/shard_map/reduce_scatter | solution.py:360
  1250.2 176.5 %reduce-scatter.47.cloned.1.call-start = ((), (), s32[]{:S(2)}) async-start(), calls=%async_computation.30 | async-start | bytes 1114112 | tf_op jit(solution)/shard_map/reduce_scatter | solution.py:360
  1255.0 234.2 %reduce-scatter.45.cloned.1.call-start = ((), (), s32[]{:S(2)}) async-start(), calls=%async_computation.29 | async-start | bytes 1114112 | tf_op jit(solution)/shard_map/reduce_scatter | solution.py:357
  1258.7 292.9 %reduce-scatter.43.cloned.1.call-start = ((), (), s32[]{:S(2)}) async-start(), calls=%async_computation.28 | async-start | bytes 1114112 | tf_op jit(solution)/shard_map/reduce_scatter | solution.py:357
  1263.0 349.6 %reduce-scatter.41.cloned.1.call-start = ((), (), s32[]{:S(2)}) async-start(), calls=%async_computation.27 | async-start | bytes 278528 | tf_op jit(solution)/shard_map/reduce_scatter | solution.py:354
  1264.8 409.0 %reduce-scatter.39.cloned.1.call-start = ((), (), s32[]{:S(2)}) async-start(), calls=%async_computation.26 | async-start | bytes 278528 | tf_op jit(solution)/shard_map/reduce_scatter | solution.py:354
  1305.0 430.9 %reduce-scatter.37.cloned.1.call-start = ((), (), s32[]{:S(2)}) async-start(), calls=%async_computation.25 | async-start | bytes 835584 | tf_op jit(solution)/shard_map/reduce_scatter | solution.py:351
  1308.9 488.8 %reduce-scatter.35.cloned.1.call-start = ((), (), s32[]{:S(2)}) async-start(), calls=%async_computation.24 | async-start | bytes 835584 | tf_op jit(solution)/shard_map/reduce_scatter | solution.py:351
  1334.4 542.1 %reduce-scatter.65.cloned.1.call-start = ((), (), s32[]{:S(2)}) async-start(), calls=%async_computation.43 | async-start | bytes 2359296
  1341.4 536.2 %copy-start.5 = (f32[1024,128]{1,0:T(8,128)S(1)}, f32[1024,128]{1,0:T(8,128)}, u32[]{:S(2)}) copy-start(f32[1024,128]{1,0:T(8,128)} %param.24) | copy-start | bytes 1572868
  1341.4 536.2 %copy-start.34 = (f32[1024]{0:T(1024)S(1)}, f32[1024]{0:T(1024)}, u32[]{:S(2)}) copy-start(f32[1024]{0:T(1024)} %copy-done.33) | copy-start | bytes 12292
  1341.4 536.2 %copy-start.36 = (f32[1024]{0:T(1024)S(1)}, f32[1024]{0:T(1024)}, u32[]{:S(2)}) copy-start(f32[1024]{0:T(1024)} %copy-done.35) | copy-start | bytes 12292
  1343.3 588.7 %copy-start.16 = (f32[1024,128]{1,0:T(8,128)S(1)}, f32[1024,128]{1,0:T(8,128)}, u32[]{:S(2)}) copy-start(f32[1024,128]{1,0:T(8,128)} %get-tuple-element.522) | copy-start | bytes 1572868
  (55 other events, 3393.9 us)
Sparse Core Ops, SparseCore 0:
  64.9 51.4 all-gather.22
  138.8 73.6 reduce-scatter.50
  432.0 57.1 all-gather.26
  513.0 73.6 reduce-scatter.54
  709.0 81.7 reduce-scatter.56
  794.5 73.8 reduce-scatter.58
  980.1 74.1 reduce-scatter.60
  1146.5 74.2 reduce-scatter.62
Sparse Core Ops, SparseCore 1:
  141.6 31.1 all-gather.38
  236.4 56.1 all-gather.24
  294.9 31.2 all-gather.40
  332.2 75.8 reduce-scatter.52
  516.0 31.1 all-gather.42
  610.6 56.1 all-gather.28
  669.0 31.2 all-gather.44
  702.9 58.4 all-gather.30
  894.6 56.1 all-gather.32
  1079.1 56.1 all-gather.34
  1245.5 56.1 all-gather.36
  1304.2 60.2 reduce-scatter.48
  1366.7 59.9 reduce-scatter.46
  1429.2 59.9 reduce-scatter.44
  1491.6 60.0 reduce-scatter.42
  1554.1 58.4 reduce-scatter.40
  1614.9 58.7 reduce-scatter.38
  1676.2 59.6 reduce-scatter.36
  1738.1 59.5 reduce-scatter.34
  1801.9 74.5 reduce-scatter.64
where the time goes:
time: 1950 us; the launch traced here: 1940 us
  waiting for transfers between devices  1340 us (69%)
  blocking collectives  346 us (18%)
  matrix products  111 us (6%)
  local copies, waits for them, and re-layouts  63.3 us (3%)
  other arithmetic  43.3 us (2%)
  between operations  19.7 us (1%)
    unnamed x36, waiting for transfers between devices  521 us
    all_gather x4, waiting for transfers between devices, gather_grads(): return lax.all_gather(rounded, 'col', axis=1, tiled=True)  201 us
    psum x8, blocking collectives, feature_sums(): return lax.psum((first_sum, second_sum), 'col')  175 us
    reduce_scatter x2, waiting for transfers between devices, layer_backward(): lax.psum_scatter(up_weight_grad.astype(jnp.bfloat16), 'row', scatter_dime...  123 us
    reduce_scatter x2, waiting for transfers between devices, layer_backward(): lax.psum_scatter(joined_weight_grad.astype(jnp.bfloat16), 'row', scatter_...  123 us
    reduce_scatter x2, waiting for transfers between devices, layer_backward(): lax.psum_scatter(out_weight_grad.astype(jnp.bfloat16), 'row', scatter_dim...  120 us
    all_gather x4, waiting for transfers between devices, gather_features(): return lax.all_gather(rounded, 'col', axis=1, tiled=True)  112 us
    reduce_scatter x2, waiting for transfers between devices, layer_backward(): lax.psum_scatter(down_weight_grad.astype(jnp.bfloat16), 'row', scatter_di...  83.2 us
  transfers between devices with their start and end apart: 28, of which 26 were waited for; matrix products, arithmetic and copies ran while one was open for 5% of the time, Pallas kernels for 0%

commit v1 on v0

v1 whole, which is shorter than its diff:
```python
import functools

import jax
import jax.numpy as jnp
from jax import lax
from jax.experimental import pallas as pl
from jax.experimental.pallas import tpu as pltpu
from jax.sharding import PartitionSpec as P

D = 1024
HEADS = 16
HDIM = 64
FF = 4096
LAYERS = 2
CAP = 1024
PARTS = 8
ROWS = CAP // PARTS
LOCAL_HEADS = HEADS // PARTS
EPS = 1e-05
NEG = -1000000000.0
MESH = pl.DeviceIdType.MESH


def place():
    row = lax.axis_index("row")
    col = lax.axis_index("col")
    return (
        lax.div(col, 4),
        lax.rem(col, 4),
        lax.div(row, 8),
        lax.div(lax.rem(row, 8), 2),
        lax.rem(row, 2),
    )


def device(h, x, zl, y, c):
    return (zl * 8 + y * 2 + c, h * 4 + x)


def turn(value, by, size):
    return lax.rem(value + by, size)


def rows_at(start, size):
    return pl.ds(pl.multiple_of(start, size), size)


def push(src, dst, send_sem, recv_sem, target):
    return pltpu.make_async_remote_copy(
        src_ref=src,
        dst_ref=dst,
        send_sem=send_sem,
        recv_sem=recv_sem,
        device_id=target,
        device_id_type=MESH,
    )


def greet(target):
    pl.semaphore_signal(
        pltpu.get_barrier_semaphore(), inc=1, device_id=target, device_id_type=MESH
    )


def await_greetings(count):
    pl.semaphore_wait(pltpu.get_barrier_semaphore(), count)


def unless(flag, run):
    pl.when(jnp.logical_not(flag))(run)


def together(*parts):
    alive = list(parts)
    while alive:
        alive = [part for part in alive if next(part, alive) is not alive]


def landed(view, send_sem, recv_sem):
    row, col = lax.axis_index("row"), lax.axis_index("col")
    push(view, view, send_sem, recv_sem, (row, lax.rem(col + 1, 8))).wait_recv()


def neighbours(where):
    h, x, zl, y, c = where
    return (
        device(h, turn(x, 1, 4), zl, y, c),
        device(h, turn(x, 3, 4), zl, y, c),
        device(h, x, zl, y, 1 - c),
    )


def greet_line(where):
    for other in neighbours(where):
        greet(other)
    return 3


def greet_ring(where, inward):
    h, x, zl, y, c = where
    home = lax.rem(h + c, 2) == 0
    for d in range(2):
        if inward:
            source = device(c, x, zl, y, turn(c, d, 2))
        else:
            source = device(turn(h, d, 2), x, zl, y, h)
        if d == 0:
            unless(home, functools.partial(greet, source))
        else:
            greet(source)
    for step in (1, 3):
        greet(device(h, x, zl, turn(y, step, 4), c))
    greet(device(h, x, 1 - zl, y, c))
    return 4 + lax.rem(h + c, 2)


def greet_swap(where, inward):
    h, x, zl, y, c = where
    home = lax.rem(h + c, 2) == 0
    for j in range(4):
        for d in range(2):
            if inward:
                source = device(turn(h, d, 2), turn(x, j, 4), zl, y, h)
            else:
                source = device(c, turn(x, j, 4), zl, y, turn(c, d, 2))
            if j == 0 and d == 0:
                unless(home, functools.partial(greet, source))
            else:
                greet(source)
    return 7 + lax.rem(h + c, 2)


def greet_parts(where):
    h, x, zl, y, c = where
    for j in range(4):
        for d in range(2):
            if j or d:
                greet(device(h, turn(x, j, 4), zl, y, turn(c, d, 2)))
    return 7


def move(src, dst, send_sem, recv_sem, target, home):
    unless(home, push(src, dst, send_sem, recv_sem, target).start)
    pl.when(home)(lambda: pltpu.make_async_copy(src, dst, recv_sem).start())


def moved_in(dst, send_sem, recv_sem, home):
    unless(home, functools.partial(landed, dst, send_sem, recv_sem))
    pl.when(home)(lambda: pltpu.make_async_copy(dst, dst, recv_sem).wait())


def moved_out(src, send_sem, recv_sem, target, home):
    unless(home, push(src, src, send_sem, recv_sem, target).wait_send)


def gather_line(where, src, out, own_sem, send, recv):
    h, x, zl, y, c = where
    right, left, mate = neighbours(where)
    half = ROWS // 2

    def block(core, step, first=0, size=ROWS):
        return out.at[rows_at((core * 4 + turn(x, step, 4)) * ROWS + first, size)]

    started = []

    def copy(index, view, target, source=None):
        source = view if source is None else source
        item = push(source, view, send.at[index], recv.at[index], target)
        item.start()
        started.append(item)

    def arrived(index, view):
        landed(view, send.at[index], recv.at[index])

    own = pltpu.make_async_copy(src, block(c, 0), own_sem)
    own.start()
    low, high = src.at[pl.ds(0, half)], src.at[pl.ds(half, half)]
    copy(0, block(c, 0, 0, half), right, low)
    copy(2, block(c, 0, half, half), left, high)
    copy(1, block(c, 0, half, half), right, high)
    copy(3, block(c, 0, 0, half), left, low)
    copy(4, block(c, 0), mate, src)
    yield
    arrived(0, block(c, 3, 0, half))
    copy(5, block(c, 3, 0, half), right)
    arrived(2, block(c, 1, half, half))
    copy(6, block(c, 1, half, half), left)
    yield
    arrived(1, block(c, 3, half, half))
    copy(7, block(c, 3), mate)
    arrived(3, block(c, 1, 0, half))
    copy(8, block(c, 1), mate)
    yield
    arrived(5, block(c, 2, 0, half))
    copy(9, block(c, 2, 0, half), mate)
    arrived(6, block(c, 2, half, half))
    copy(10, block(c, 2, half, half), mate)
    yield
    arrived(4, block(1 - c, 0))
    arrived(7, block(1 - c, 3))
    arrived(8, block(1 - c, 1))
    arrived(9, block(1 - c, 2, 0, half))
    arrived(10, block(1 - c, 2, half, half))
    for item in started:
        item.wait_send()
    own.wait()


LINE_SEMS = [
    pltpu.SemaphoreType.DMA,
    pltpu.SemaphoreType.DMA((11,)),
    pltpu.SemaphoreType.DMA((11,)),
]
RING_SEMS = [pltpu.SemaphoreType.DMA((9,)), pltpu.SemaphoreType.DMA((9,))]


def spread_line(where, part, out, core_in, sums, hop, final, send, recv):
    h, x, zl, y, c = where
    right, left, mate = neighbours(where)
    half = ROWS // 2
    low, high = pl.ds(0, half), pl.ds(half, half)

    def mine(core, step):
        return part.at[rows_at((core * 4 + turn(x, step, 4)) * ROWS, ROWS)]

    started = []

    def copy(index, source, view, target):
        item = push(source, view, send.at[index], recv.at[index], target)
        item.start()
        started.append(item)

    def arrived(index, view):
        landed(view, send.at[index], recv.at[index])

    for index, step in enumerate((2, 1, 3, 0)):
        copy(index, mine(1 - c, step), core_in.at[step], mate)
    yield

    def core_sum(step):
        return mine(c, step)[...].astype(jnp.float32) + core_in[step].astype(jnp.float32)

    arrived(0, core_in.at[2])
    sums[2] = core_sum(2).astype(jnp.bfloat16)
    copy(4, sums.at[2, low], hop.at[0], right)
    copy(5, sums.at[2, high], hop.at[1], left)
    arrived(1, core_in.at[1])
    sums[1] = core_sum(1).astype(jnp.bfloat16)
    copy(6, sums.at[1, high], final.at[0, high], right)
    arrived(2, core_in.at[3])
    sums[3] = core_sum(3).astype(jnp.bfloat16)
    copy(7, sums.at[3, low], final.at[1, low], left)
    yield
    arrived(3, core_in.at[0])
    out[...] = core_sum(0)
    arrived(4, hop.at[0])
    sums[1, :half] = (sums[1, :half].astype(jnp.float32) + hop[0].astype(jnp.float32)).astype(
        jnp.bfloat16
    )
    copy(8, sums.at[1, low], final.at[0, low], right)
    arrived(5, hop.at[1])
    sums[3, half:] = (sums[3, half:].astype(jnp.float32) + hop[1].astype(jnp.float32)).astype(
        jnp.bfloat16
    )
    copy(9, sums.at[3, high], final.at[1, high], left)
    yield
    arrived(6, final.at[0, high])
    arrived(7, final.at[1, low])
    yield
    arrived(8, final.at[0, low])
    arrived(9, final.at[1, high])
    out[...] += final[0].astype(jnp.float32) + final[1].astype(jnp.float32)
    for item in started:
        item.wait_send()


def spread_scratch():
    half = ROWS // 2
    return [
        pltpu.VMEM((4, ROWS, D), jnp.bfloat16),
        pltpu.VMEM((4, ROWS, D), jnp.bfloat16),
        pltpu.VMEM((2, half, D), jnp.bfloat16),
        pltpu.VMEM((2, ROWS, D), jnp.bfloat16),
        pltpu.SemaphoreType.DMA((10,)),
        pltpu.SemaphoreType.DMA((10,)),
    ]


def gather_ring(where, own, slot, send, recv):
    h, x, zl, y, c = where
    home = lax.rem(h + c, 2) == 0
    above = device(h, x, zl, turn(y, 1, 4), c)
    below = device(h, x, zl, turn(y, 3, 4), c)
    beside = device(h, x, 1 - zl, y, c)

    def piece(p, step):
        return slot(turn(zl, p, 2), turn(y, step, 4), 0, 2, c)

    def ring(index, view, target):
        push(view, view, send.at[index], recv.at[index], target).start()

    def arrived(index, view):
        landed(view, send.at[index], recv.at[index])

    for d in range(2):
        target = device(turn(h, d, 2), x, zl, y, h)
        args = (own, slot(zl, y, c, 1, h), send.at[d], recv.at[c], target)
        if d == 0:
            move(*args, home)
        else:
            push(*args).start()
    yield
    for d in range(2):
        cc = turn(c, d, 2)
        args = (slot(zl, y, cc, 1, c), send.at[d], recv.at[cc])
        if d == 0:
            moved_in(*args, home)
        else:
            landed(*args)
    ring(2, piece(0, 0), beside)
    ring(3, piece(0, 0), above)
    ring(5, piece(0, 0), below)
    yield
    arrived(2, piece(1, 0))
    ring(4, piece(1, 0), above)
    ring(6, piece(1, 0), below)
    yield
    arrived(3, piece(0, 3))
    ring(7, piece(0, 3), above)
    arrived(6, piece(1, 1))
    ring(8, piece(1, 1), below)
    yield
    arrived(4, piece(1, 3))
    arrived(5, piece(0, 1))
    arrived(7, piece(0, 2))
    arrived(8, piece(1, 2))
    moved_out(own, send.at[0], recv.at[0], beside, home)
    push(own, own, send.at[1], recv.at[1], beside).wait_send()
    for index in range(2, 9):
        push(piece(0, 0), piece(0, 0), send.at[index], recv.at[index], beside).wait_send()


def gather_parts(where, block, send, recv):
    h, x, zl, y, c = where
    pairs = [(j, d) for j in range(4) for d in range(2) if j or d]
    mine = c * 4 + x
    started = []
    for index, (j, d) in enumerate(pairs):
        target = device(h, turn(x, j, 4), zl, y, turn(c, d, 2))
        item = push(block(mine), block(mine), send.at[index], recv.at[mine], target)
        item.start()
        started.append(item)
    yield
    for index, (j, d) in enumerate(pairs):
        other = turn(c, d, 2) * 4 + turn(x, j, 4)
        landed(block(other), send.at[index], recv.at[other])
    for item in started:
        item.wait_send()


def one_after_other(*parts):
    for part in parts:
        yield from part


def swap_in(where, pairs, send, recv):
    h, x, zl, y, c = where
    home = lax.rem(h + c, 2) == 0
    mine = h * 4 + x
    for item, (src, dst) in enumerate(pairs):
        for j in range(4):
            for d in range(2):
                xx, cc = turn(x, j, 4), turn(c, d, 2)
                args = (
                    src.at[rows_at((cc * 4 + xx) * ROWS, ROWS)],
                    dst.at[:, rows_at(mine * 128, 128)],
                    send.at[item, j * 2 + d],
                    recv.at[item, mine],
                    device(c, xx, zl, y, cc),
                )
                if j or d:
                    push(*args).start()
                else:
                    move(*args, home)
    yield
    for item, (src, dst) in enumerate(pairs):
        for j in range(4):
            for d in range(2):
                k = turn(h, d, 2) * 4 + turn(x, j, 4)
                view = dst.at[:, rows_at(k * 128, 128)]
                sems = (send.at[item, j * 2 + d], recv.at[item, k])
                gone = src.at[pl.ds(0, ROWS)]
                other = device(h, x, 1 - zl, y, c)
                if j or d:
                    landed(view, *sems)
                    push(gone, gone, *sems, other).wait_send()
                else:
                    moved_in(view, *sems, home)
                    moved_out(gone, *sems, other, home)


def swap_out(where, pairs, send, recv):
    h, x, zl, y, c = where
    home = lax.rem(h + c, 2) == 0
    mine = c * 4 + x
    for item, (src, dst) in enumerate(pairs):
        for j in range(4):
            for d in range(2):
                hh, xx = turn(h, d, 2), turn(x, j, 4)
                args = (
                    src.at[:, rows_at((hh * 4 + xx) * 128, 128)],
                    dst.at[rows_at(mine * ROWS, ROWS)],
                    send.at[item, j * 2 + d],
                    recv.at[item, mine],
                    device(hh, xx, zl, y, h),
                )
                if j or d:
                    push(*args).start()
                else:
                    move(*args, home)
    yield
    for item, (src, dst) in enumerate(pairs):
        for j in range(4):
            for d in range(2):
                part = turn(c, d, 2) * 4 + turn(x, j, 4)
                view = dst.at[rows_at(part * ROWS, ROWS)]
                sems = (send.at[item, j * 2 + d], recv.at[item, part])
                gone = src.at[:, pl.ds(0, 128)]
                other = device(h, x, 1 - zl, y, c)
                if j or d:
                    landed(view, *sems)
                    push(gone, gone, *sems, other).wait_send()
                else:
                    moved_in(view, *sems, home)
                    moved_out(gone, *sems, other, home)


def scatter_ring(where, rows, depth, out, hop, final, sums, kept, across, pair, last, send, recv):
    h, x, zl, y, c = where
    home = lax.rem(h + c, 2) == 0
    above = device(h, x, zl, turn(y, 1, 4), c)
    below = device(h, x, zl, turn(y, 3, 4), c)
    beside = device(h, x, 1 - zl, y, c)
    kind = hop.dtype

    def piece(p, step):
        return rows((turn(zl, p, 2) * 8 + turn(y, step, 4) * 2) * depth, 2 * depth)

    def wide(value):
        return value.astype(jnp.float32)

    def go(index, src, dst, target):
        push(src, dst, send.at[index], recv.at[index], target).start()

    def come(index, dst):
        landed(dst, send.at[index], recv.at[index])

    go(0, piece(0, 2), hop.at[0], above)
    go(1, piece(1, 2), hop.at[1], below)
    go(2, piece(1, 1), final.at[0, 1], above)
    go(3, piece(0, 3), final.at[1, 0], below)
    yield
    come(0, hop.at[0])
    sums[0] = (wide(piece(0, 1)[...]) + wide(hop[0])).astype(kind)
    go(4, sums.at[0], final.at[0, 0], above)
    come(1, hop.at[1])
    sums[1] = (wide(piece(1, 3)[...]) + wide(hop[1])).astype(kind)
    go(5, sums.at[1], final.at[1, 1], below)
    yield
    come(2, final.at[0, 1])
    come(5, final.at[1, 1])
    across[0] = (wide(piece(1, 0)[...]) + wide(final[0, 1]) + wide(final[1, 1])).astype(kind)
    go(6, across.at[0], across.at[1], beside)
    come(3, final.at[1, 0])
    come(4, final.at[0, 0])
    kept[...] = wide(piece(0, 0)[...]) + wide(final[0, 0]) + wide(final[1, 0])
    yield
    come(6, across.at[1])
    pair[...] = (kept[...] + wide(across[1])).astype(kind)
    for d in range(2):
        cc = turn(c, d, 2)
        args = (
            pair.at[rows_at(cc * depth, depth)],
            last.at[h],
            send.at[7 + d],
            recv.at[7 + h],
            device(c, x, zl, y, cc),
        )
        if d == 0:
            move(*args, home)
        else:
            push(*args).start()
    yield
    for d in range(2):
        hh = turn(h, d, 2)
        args = (last.at[hh], send.at[7 + d], recv.at[7 + hh])
        if d == 0:
            moved_in(*args, home)
        else:
            landed(*args)
    out[...] = wide(last[0]) + wide(last[1])
    for index in range(7):
        push(piece(0, 0), piece(0, 0), send.at[index], recv.at[index], beside).wait_send()
    gone = pair.at[pl.ds(0, depth)]
    moved_out(gone, send.at[7], recv.at[7], beside, home)
    push(gone, gone, send.at[8], recv.at[8], beside).wait_send()


def scatter_scratch(depth, rest, kind):
    both = (2 * depth,) + rest
    return [
        pltpu.VMEM((2,) + both, kind),
        pltpu.VMEM((2, 2) + both, kind),
        pltpu.VMEM((2,) + both, kind),
        pltpu.VMEM(both, jnp.float32),
        pltpu.VMEM((2,) + both, kind),
        pltpu.VMEM(both, kind),
        pltpu.VMEM((2, depth) + rest, kind),
    ] + RING_SEMS


def rows_of(full, depth):
    def slot(zz, yy, cc, count, core):
        return full.at[rows_at((zz * 8 + yy * 2 + cc) * depth, depth * count)]

    return slot


def rows_view(ref):
    return lambda start, count: ref.at[rows_at(start, count)]


ANYWHERE = pl.BlockSpec(memory_space=pl.ANY)
INSIDE = pl.BlockSpec(memory_space=pltpu.VMEM)
DEPTH = D // 16
CHUNK = 512


def call(body, name, number, ins, outs, scratch, args):
    result = pl.pallas_call(
        body,
        out_shape=tuple(shape for shape, _ in outs),
        in_specs=ins,
        out_specs=tuple(spec for _, spec in outs),
        scratch_shapes=scratch,
        compiler_params=pltpu.CompilerParams(
            collective_id=number, has_side_effects=True, vmem_limit_bytes=40 * 2**20
        ),
        name=name,
    )(*args)
    return result


FULL_ROWS = jax.ShapeDtypeStruct((CAP, D), jnp.bfloat16)
FULL_CHUNK = jax.ShapeDtypeStruct((D, CHUNK), jnp.bfloat16)
OWN_CHUNK = jax.ShapeDtypeStruct((DEPTH, CHUNK), jnp.float32)
OWN_ROWS = jax.ShapeDtypeStruct((ROWS, D), jnp.float32)


def gather_rows(rows, weights=None, grads=None):
    if weights is not None:

        def body(src, own, out, full, *sems):
            where = place()
            await_greetings(greet_line(where) + greet_ring(where, True))
            together(
                gather_line(where, src, out, *sems[:3]),
                gather_ring(where, own, rows_of(full, DEPTH), *sems[3:]),
            )

        return call(
            body,
            "gather_rows_weights",
            1,
            [ANYWHERE] * 2,
            [(FULL_ROWS, ANYWHERE), (FULL_CHUNK, ANYWHERE)],
            LINE_SEMS + RING_SEMS,
            (rows, weights),
        )
    if grads is not None:

        def body(src, part, out, own, *scratch):
            where = place()
            await_greetings(greet_line(where) + greet_ring(where, False))
            together(
                scatter_ring(where, rows_view(part), DEPTH, own, *scratch[3:]),
                gather_line(where, src, out, *scratch[:3]),
            )

        return call(
            body,
            "gather_rows_grads",
            2,
            [ANYWHERE, INSIDE],
            [(FULL_ROWS, ANYWHERE), (OWN_CHUNK, INSIDE)],
            LINE_SEMS + scatter_scratch(DEPTH, (CHUNK,), jnp.bfloat16),
            (rows, grads),
        )

    def body(src, out, *sems):
        where = place()
        await_greetings(greet_line(where))
        together(gather_line(where, src, out, *sems))

    return call(body, "gather_rows", 3, [ANYWHERE], [(FULL_ROWS, ANYWHERE)], LINE_SEMS, (rows,))[0]


def spread_rows(part, weights=None, grads=None):
    count = len(spread_scratch())
    if weights is not None:

        def body(part, own, out, full, *scratch):
            where = place()
            await_greetings(greet_line(where) + greet_ring(where, True))
            together(
                spread_line(where, part, out, *scratch[:count]),
                gather_ring(where, own, rows_of(full, DEPTH), *scratch[count:]),
            )

        return call(
            body,
            "spread_rows_weights",
            4,
            [INSIDE, ANYWHERE],
            [(OWN_ROWS, INSIDE), (FULL_CHUNK, ANYWHERE)],
            spread_scratch() + RING_SEMS,
            (part, weights),
        )
    if grads is not None:

        def body(part, grads, out, own, *scratch):
            where = place()
            await_greetings(greet_line(where) + greet_ring(where, False))
            together(
                spread_line(where, part, out, *scratch[:count]),
                scatter_ring(where, rows_view(grads), DEPTH, own, *scratch[count:]),
            )

        return call(
            body,
            "spread_rows_grads",
            5,
            [INSIDE, INSIDE],
            [(OWN_ROWS, INSIDE), (OWN_CHUNK, INSIDE)],
            spread_scratch() + scatter_scratch(DEPTH, (CHUNK,), jnp.bfloat16),
            (part, grads),
        )

    def body(part, out, *scratch):
        where = place()
        await_greetings(greet_line(where))
        together(spread_line(where, part, out, *scratch))

    return call(
        body, "spread_rows", 6, [INSIDE], [(OWN_ROWS, INSIDE)], spread_scratch(), (part,)
    )[0]


def enter_body(
    hid, cot, weights, pack, hid_out, cot_out, full, packs,
    ring_send, ring_recv, pack_send, pack_recv, part_send, part_recv, swap_send, swap_recv,
):
    where = place()
    h, x, zl, y, c = where
    await_greetings(greet_swap(where, True) + greet_ring(where, True) + greet_parts(where))

    def pack_slot(zz, yy, cc, count, core):
        return packs.at[core * 4 + x, pl.ds(zz * 8 + yy * 2 + cc, count)]

    together(
        one_after_other(
            gather_ring(where, pack, pack_slot, pack_send, pack_recv),
            gather_parts(where, lambda part: packs.at[part], part_send, part_recv),
        ),
        gather_ring(where, weights, rows_of(full, DEPTH), ring_send, ring_recv),
        swap_in(where, ((hid, hid_out), (cot, cot_out)), swap_send, swap_recv),
    )


def enter(hidden, cotangent, weights, pack):
    return call(
        enter_body,
        "enter",
        0,
        [ANYWHERE] * 4,
        [
            (OWN_ROWS, ANYWHERE),
            (OWN_ROWS, ANYWHERE),
            (FULL_CHUNK, ANYWHERE),
            (jax.ShapeDtypeStruct((8, 16, 1, 256), jnp.float32), ANYWHERE),
        ],
        RING_SEMS + RING_SEMS
        + [pltpu.SemaphoreType.DMA((7,)), pltpu.SemaphoreType.DMA((8,))]
        + [pltpu.SemaphoreType.DMA((2, 8)), pltpu.SemaphoreType.DMA((2, 8))],
        (hidden, cotangent, weights, pack),
    )


def leave_body(hid, cot, grads, vectors, hid_out, cot_out, out, vector_out, *scratch):
    where = place()
    h, x, zl, y, c = where
    await_greetings(greet_swap(where, False) + greet_ring(where, False) + greet_parts(where))
    ring, rest = scratch[:9], scratch[9:]
    vector_ring, rest = rest[:9], rest[9:]
    taken, total, part_send, part_recv, swap_send, swap_recv = rest

    def vector_parts():
        pairs = [(j, d) for j in range(4) for d in range(2) if j or d]
        mine = c * 4 + x
        started = []
        for index, (j, d) in enumerate(pairs):
            xx, cc = turn(x, j, 4), turn(c, d, 2)
            item = push(
                vectors.at[cc * 4 + xx],
                taken.at[index],
                part_send.at[index],
                part_recv.at[index],
                device(h, xx, zl, y, cc),
            )
            item.start()
            started.append(item)
        yield
        value = vectors[mine]
        for index in range(7):
            landed(taken.at[index], part_send.at[index], part_recv.at[index])
            value = value + taken[index]
        total[...] = value
        for item in started:
            item.wait_send()
        yield from scatter_ring(
            where, lambda start, count: total.at[pl.ds(start, count)], 1, vector_out, *vector_ring
        )

    together(
        scatter_ring(where, rows_view(grads), DEPTH, out, *ring),
        vector_parts(),
        swap_out(where, ((hid, hid_out), (cot, cot_out)), swap_send, swap_recv),
    )


def leave(hidden, grad_hidden, grads, vectors):
    columns = jax.ShapeDtypeStruct((CAP, 128), jnp.float32)
    return call(
        leave_body,
        "leave",
        7,
        [ANYWHERE, ANYWHERE, INSIDE, INSIDE],
        [
            (columns, ANYWHERE),
            (columns, ANYWHERE),
            (OWN_CHUNK, INSIDE),
            (jax.ShapeDtypeStruct((1, 1, 256), jnp.float32), INSIDE),
        ],
        scatter_scratch(DEPTH, (CHUNK,), jnp.bfloat16)
        + scatter_scratch(1, (1, 256), jnp.float32)
        + [
            pltpu.VMEM((7, 16, 1, 256), jnp.float32),
            pltpu.VMEM((16, 1, 256), jnp.float32),
            pltpu.SemaphoreType.DMA((7,)),
            pltpu.SemaphoreType.DMA((7,)),
            pltpu.SemaphoreType.DMA((2, 8)),
            pltpu.SemaphoreType.DMA((2, 8)),
        ],
        (hidden, grad_hidden, grads, vectors),
    )


def gelu_tanh(values):
    return (
        0.5
        * values
        * (1.0 + jnp.tanh(0.7978845608028654 * (values + 0.044715 * values * values * values)))
    )


def dot(left, right):
    return jnp.dot(left, right, preferred_element_type=jnp.float32)


def dot_t(left, right):
    return lax.dot_general(left, right, (((1,), (1,)), ((), ())), preferred_element_type=jnp.float32)


def t_dot(left, right):
    return lax.dot_general(left, right, (((0,), (0,)), ((), ())), preferred_element_type=jnp.float32)


def norm_forward(hidden, gain, shift):
    centred = hidden - jnp.mean(hidden, axis=1, keepdims=True)
    inverse = lax.rsqrt(jnp.mean(centred * centred, axis=1, keepdims=True) + EPS)
    normed = centred * inverse
    return (normed, inverse, (normed * gain + shift).astype(jnp.bfloat16))


def norm_backward(grad_rows, normed, inverse, gain):
    grad_gain = jnp.sum(grad_rows * normed, axis=0)
    grad_shift = jnp.sum(grad_rows, axis=0)
    scaled = grad_rows * gain
    mean_one = jnp.mean(scaled, axis=1, keepdims=True)
    mean_two = jnp.mean(scaled * normed, axis=1, keepdims=True)
    return (inverse * (scaled - mean_one - normed * mean_two), grad_gain, grad_shift)


def block_scores(query_block, key_rows, first_row, segment, slopes, score_scale):
    block_rows = query_block.shape[0]
    row_index = first_row + jnp.arange(block_rows, dtype=jnp.int32)
    columns = jnp.arange(key_rows.shape[0], dtype=jnp.int32)
    offset = (columns[None, :] - row_index[:, None]).astype(jnp.float32)
    scores = (
        jnp.einsum("qhd,khd->hqk", query_block, key_rows, preferred_element_type=jnp.float32)
        * score_scale
    )
    scores = scores + slopes[:, None, None] * offset[None]
    row_segment = lax.dynamic_slice_in_dim(segment, first_row, block_rows)
    allowed = (row_segment[:, None] == segment[None, :]) & (columns[None, :] <= row_index[:, None])
    return jnp.where(allowed[None], scores, NEG)


def attend_forward(query_rows, key_rows, value_rows, segment, slopes, score_scale, block_rows):
    block_count = query_rows.shape[0] // block_rows

    def one_block(block_index):
        first_row = block_index * block_rows
        query_block = lax.dynamic_slice_in_dim(query_rows, first_row, block_rows)
        scores = block_scores(query_block, key_rows, first_row, segment, slopes, score_scale)
        row_max = jnp.max(scores, axis=-1, keepdims=True)
        shifted = jnp.exp(scores - row_max)
        row_total = jnp.sum(shifted, axis=-1, keepdims=True)
        soft_probs = (shifted / row_total).astype(jnp.bfloat16)
        mixed_block = jnp.einsum(
            "hqk,khd->qhd", soft_probs, value_rows, preferred_element_type=jnp.float32
        )
        return (mixed_block.astype(jnp.bfloat16), (row_max + jnp.log(row_total))[..., 0])

    mixed_heads, log_totals = lax.map(one_block, jnp.arange(block_count, dtype=jnp.int32))
    return (mixed_heads.reshape(query_rows.shape), log_totals)


def attend_backward(
    query_rows,
    key_rows,
    value_rows,
    grad_heads,
    log_totals,
    segment,
    slopes,
    score_scale,
    block_rows,
):
    block_count = query_rows.shape[0] // block_rows

    def one_block(carried, block_index):
        grad_keys, grad_values = carried
        first_row = block_index * block_rows
        query_block = lax.dynamic_slice_in_dim(query_rows, first_row, block_rows)
        grad_block = lax.dynamic_slice_in_dim(grad_heads, first_row, block_rows)
        scores = block_scores(query_block, key_rows, first_row, segment, slopes, score_scale)
        soft_probs = jnp.exp(scores - log_totals[block_index][..., None])
        grad_probs = jnp.einsum(
            "qhd,khd->hqk", grad_block, value_rows, preferred_element_type=jnp.float32
        )
        inner_sum = jnp.sum(soft_probs * grad_probs, axis=-1, keepdims=True)
        grad_scores = (soft_probs * (grad_probs - inner_sum)).astype(jnp.bfloat16)
        grad_query = (
            jnp.einsum("hqk,khd->qhd", grad_scores, key_rows, preferred_element_type=jnp.float32)
            * score_scale
        )
        grad_keys = (
            grad_keys
            + jnp.einsum(
                "hqk,qhd->khd", grad_scores, query_block, preferred_element_type=jnp.float32
            )
            * score_scale
        )
        grad_values = grad_values + jnp.einsum(
            "hqk,qhd->khd",
            soft_probs.astype(jnp.bfloat16),
            grad_block,
            preferred_element_type=jnp.float32,
        )
        return ((grad_keys, grad_values), grad_query)

    zero_rows = jnp.zeros(key_rows.shape, jnp.float32)
    (grad_keys, grad_values), grad_queries = lax.scan(
        one_block, (zero_rows, zero_rows), jnp.arange(block_count, dtype=jnp.int32)
    )
    return (grad_queries.reshape(query_rows.shape), grad_keys, grad_values)


def layer_forward(hidden, weights, vectors, segment, slopes, part, cargo):
    (first_gain, first_shift, query_bias, value_bias, out_bias, second_gain, second_shift, down_bias, up_bias) = vectors
    joined_out = weights["joined_out"]
    normed_one, inverse_one, first_rows = norm_forward(hidden, first_gain, first_shift)
    first_full = carry(gather_rows, first_rows, cargo[0])
    joined_rows = dot(first_full, joined_out[:, :384]).reshape(CAP, LOCAL_HEADS, 3, HDIM)
    query_rows = (joined_rows[:, :, 0] + query_bias.reshape(LOCAL_HEADS, HDIM)).astype(jnp.bfloat16)
    key_rows = joined_rows[:, :, 1].astype(jnp.bfloat16)
    value_rows = (joined_rows[:, :, 2] + value_bias.reshape(LOCAL_HEADS, HDIM)).astype(jnp.bfloat16)
    mixed_heads, log_totals = attend_forward(
        query_rows, key_rows, value_rows, segment, slopes, HDIM ** (-0.5), 512
    )
    heads_flat = mixed_heads.reshape(CAP, -1)
    branch = carry(spread_rows, dot_t(heads_flat, joined_out[:, 384:]).astype(jnp.bfloat16), cargo[1])
    middle = hidden + branch + out_bias
    normed_two, inverse_two, second_rows = norm_forward(middle, second_gain, second_shift)
    second_full = carry(gather_rows, second_rows, cargo[2])
    up_rows = dot(second_full, weights["up"]) + up_bias
    activated = gelu_tanh(up_rows).astype(jnp.bfloat16)
    down_rows = carry(spread_rows, dot_t(activated, weights["down"]).astype(jnp.bfloat16), cargo[3])
    saved_rows = (
        normed_one,
        inverse_one,
        first_full,
        query_rows,
        key_rows,
        value_rows,
        log_totals,
        heads_flat,
        normed_two,
        inverse_two,
        second_full,
        up_rows,
        activated,
    )
    return (middle + down_rows + down_bias, saved_rows)


def carry(transfer, rows, cargo):
    if cargo is None:
        return transfer(rows)
    chunk, kept, name = cargo
    result, kept[name] = transfer(rows, weights=chunk)
    return result


def layer_backward(grad_next, weights, vectors, saved_rows, segment, slopes, part, waiting):
    (first_gain, first_shift, query_bias, value_bias, out_bias, second_gain, second_shift, down_bias, up_bias) = vectors
    (
        normed_one,
        inverse_one,
        first_full,
        query_rows,
        key_rows,
        value_rows,
        log_totals,
        heads_flat,
        normed_two,
        inverse_two,
        second_full,
        up_rows,
        activated,
    ) = saved_rows
    joined_out = weights["joined_out"]
    grad_down = grad_next.astype(jnp.bfloat16)
    down_bias_grad = jnp.sum(grad_down.astype(jnp.float32), axis=0)
    if waiting is None:
        grad_down_full, finished = gather_rows(grad_down), None
    else:
        grad_down_full, finished = gather_rows(grad_down, grads=waiting)
    grad_act = dot(grad_down_full, weights["down"])
    down_grad = t_dot(grad_down_full, activated).astype(jnp.bfloat16)
    _, gelu_pull = jax.vjp(gelu_tanh, up_rows)
    grad_up = gelu_pull(grad_act)[0].astype(jnp.bfloat16)
    up_bias_grad = jnp.sum(grad_up.astype(jnp.float32), axis=0)
    up_grad = t_dot(second_full, grad_up).astype(jnp.bfloat16)
    grad_second, down_sum = spread_rows(
        dot_t(grad_up, weights["up"]).astype(jnp.bfloat16), grads=down_grad
    )
    grad_norm_two, second_gain_grad, second_shift_grad = norm_backward(
        grad_second, normed_two, inverse_two, second_gain
    )
    grad_middle = grad_next + grad_norm_two
    grad_branch = grad_middle.astype(jnp.bfloat16)
    out_bias_grad = jnp.sum(grad_branch.astype(jnp.float32), axis=0)
    grad_branch_full, up_sum = gather_rows(grad_branch, grads=up_grad)
    out_grad = t_dot(grad_branch_full, heads_flat).astype(jnp.bfloat16)
    grad_heads = dot(grad_branch_full, joined_out[:, 384:]).astype(jnp.bfloat16)
    grad_heads = grad_heads.reshape(query_rows.shape)
    grad_query, grad_keys, grad_values = attend_backward(
        query_rows,
        key_rows,
        value_rows,
        grad_heads,
        log_totals,
        segment,
        slopes,
        HDIM ** (-0.5),
        512,
    )
    query_low = grad_query.astype(jnp.bfloat16)
    key_low = grad_keys.astype(jnp.bfloat16)
    value_low = grad_values.astype(jnp.bfloat16)
    query_bias_grad = jnp.sum(query_low.astype(jnp.float32), axis=0).reshape(-1)
    value_bias_grad = jnp.sum(value_low.astype(jnp.float32), axis=0).reshape(-1)
    grad_joined = jnp.stack([query_low, key_low, value_low], axis=2).reshape(CAP, -1)
    joined_grad = t_dot(first_full, grad_joined).astype(jnp.bfloat16)
    grad_first = spread_rows(dot_t(grad_joined, joined_out[:, :384]).astype(jnp.bfloat16))
    grad_norm_one, first_gain_grad, first_shift_grad = norm_backward(
        grad_first, normed_one, inverse_one, first_gain
    )
    grad_hidden = grad_middle + grad_norm_one

    def lay(piece, size):
        return lax.dynamic_update_slice(
            jnp.zeros((size,), jnp.float32), piece, (part * piece.shape[0],)
        )

    small = jnp.stack(
        [
            first_gain_grad,
            first_shift_grad,
            lay(query_bias_grad, D),
            lay(value_bias_grad, D),
            out_bias_grad,
            second_gain_grad,
            second_shift_grad,
            down_bias_grad,
        ]
    )
    sums = {"down": down_sum, "up": up_sum}
    return (
        grad_hidden,
        sums,
        jnp.concatenate([joined_grad, out_grad], axis=1),
        finished,
        small,
        lay(up_bias_grad, FF),
    )


def shards(
    hidden_in,
    joined_weight,
    query_bias,
    value_bias,
    out_weight,
    out_bias,
    first_gain,
    first_shift,
    up_weight,
    up_bias,
    down_weight,
    down_bias,
    second_gain,
    second_shift,
    seq_lengths,
    cotangent,
):
    h, x, zl, y, c = place()
    part = c * 4 + x
    small = jnp.stack(
        [
            first_gain,
            first_shift,
            query_bias,
            value_bias,
            out_bias,
            second_gain,
            second_shift,
            down_bias,
        ],
        axis=1,
    )
    pack = jnp.concatenate(
        [
            small.reshape(-1).astype(jnp.float32),
            up_bias.reshape(-1).astype(jnp.float32),
            seq_lengths[0].astype(jnp.float32),
            jnp.zeros((60,), jnp.float32),
        ]
    )
    joined_out = jnp.concatenate([joined_weight, jnp.swapaxes(out_weight, 1, 2)], axis=2)
    down_turned = jnp.swapaxes(down_weight, 1, 2)
    weights = [{} for _ in range(LAYERS)]
    hidden, grad_hidden, weights[0]["joined_out"], packs = enter(
        hidden_in, cotangent, joined_out[0], pack.reshape(1, 1, 256)
    )
    packs = packs.reshape(8, 16, 256)
    small_full = (
        packs[:, :, :128].reshape(8, 16, LAYERS, 8, 8).transpose(2, 3, 0, 1, 4).reshape(LAYERS, 8, D)
    )
    up_full = packs[:, :, 128:192].reshape(8, 16, LAYERS, 32).transpose(2, 0, 1, 3).reshape(LAYERS, FF)
    group_pack = lax.dynamic_index_in_dim(packs[0], zl * 8 + y * 2 + h, 0, keepdims=False)
    seq_ends = jnp.cumsum(group_pack[192:196].astype(jnp.int32))
    positions = jnp.arange(CAP, dtype=jnp.int32)
    segment = jnp.sum((positions[:, None] >= seq_ends[None, :]).astype(jnp.int32), axis=1)
    head_numbers = (part * LOCAL_HEADS + jnp.arange(LOCAL_HEADS, dtype=jnp.int32)).astype(jnp.float32)
    slopes = jnp.exp2(-8.0 * (head_numbers + 1.0) / HEADS)

    def vectors_of(layer):
        def own(vector, size):
            return lax.dynamic_slice_in_dim(vector, part * size, size)

        member = small_full[layer]
        return (
            member[0],
            member[1],
            own(member[2], D // PARTS),
            own(member[3], D // PARTS),
            member[4],
            member[5],
            member[6],
            member[7],
            own(up_full[layer], FF // PARTS),
        )

    to_fetch = [
        [
            (up_weight[0], weights[0], "up"),
            (down_turned[0], weights[0], "down"),
            (joined_out[1], weights[1], "joined_out"),
            (up_weight[1], weights[1], "up"),
        ],
        [(down_turned[1], weights[1], "down"), None, None, None],
    ]
    kept_rows = []
    for layer in range(LAYERS):
        hidden, saved_rows = layer_forward(
            hidden, weights[layer], vectors_of(layer), segment, slopes, part, to_fetch[layer]
        )
        kept_rows.append(saved_rows)
    sums = [None] * LAYERS
    small_grads = [None] * LAYERS
    up_bias_grads = [None] * LAYERS
    waiting = None
    for layer in range(LAYERS - 1, -1, -1):
        grad_hidden, sums[layer], left_over, finished, small_grads[layer], up_bias_grads[layer] = (
            layer_backward(
                grad_hidden,
                weights[layer],
                vectors_of(layer),
                kept_rows[layer],
                segment,
                slopes,
                part,
                waiting,
            )
        )
        if finished is not None:
            sums[layer + 1]["joined_out"] = finished
        waiting = left_over
    small_stack = (
        jnp.stack(small_grads)
        .reshape(LAYERS, 8, 8, 16, 8)
        .transpose(2, 3, 0, 1, 4)
        .reshape(8, 16, 128)
    )
    up_stack = (
        jnp.stack(up_bias_grads)
        .reshape(LAYERS, 8, 16, 32)
        .transpose(1, 2, 0, 3)
        .reshape(8, 16, 64)
    )
    vectors = jnp.concatenate(
        [small_stack, up_stack, jnp.zeros((8, 16, 64), jnp.float32)], axis=2
    ).reshape(8, 16, 1, 256)
    hidden_out, grad_out, sums[0]["joined_out"], vector_sums = leave(
        hidden, grad_hidden, waiting, vectors
    )
    small_sums = vector_sums[0, 0, :128].reshape(LAYERS, 8, 8)
    up_sums = vector_sums[0, 0, 128:192].reshape(LAYERS, 32)
    joined_sums = jnp.stack([sums[layer]["joined_out"] for layer in range(LAYERS)])
    up_weight_sums = jnp.stack([sums[layer]["up"] for layer in range(LAYERS)])
    down_sums = jnp.stack([sums[layer]["down"] for layer in range(LAYERS)])
    return (
        hidden_out,
        grad_out,
        joined_sums[:, :, :384],
        small_sums[:, 2],
        small_sums[:, 3],
        jnp.swapaxes(joined_sums[:, :, 384:], 1, 2),
        small_sums[:, 4],
        small_sums[:, 0],
        small_sums[:, 1],
        up_weight_sums,
        up_sums,
        jnp.swapaxes(down_sums, 1, 2),
        small_sums[:, 7],
        small_sums[:, 5],
        small_sums[:, 6],
    )


def solution(mesh):
    vector = P(None, ("col", "row"))
    return jax.shard_map(
        shards,
        mesh=mesh,
        in_specs=(
            P("row", "col"),
            P(None, "row", "col"),
            vector,
            vector,
            P(None, "col", "row"),
            vector,
            vector,
            vector,
            P(None, "row", "col"),
            vector,
            P(None, "col", "row"),
            vector,
            vector,
            vector,
            P("row", None),
            P("row", "col"),
        ),
        out_specs=(
            P("row", "col"),
            P("row", "col"),
            P(None, "row", "col"),
            vector,
            vector,
            P(None, "col", "row"),
            vector,
            vector,
            vector,
            P(None, "row", "col"),
            vector,
            P(None, "col", "row"),
            vector,
            vector,
            vector,
        ),
        check_vma=False,
    )
```

time: 1950 us -> 560 us (0.29)
  waiting for transfers between devices: 1340 us -> 0 us
  Pallas kernels: 0 us -> 357 us
  blocking collectives: 346 us -> 0 us
  matrix products: 111 us -> 71.8 us
    unnamed x36 -> x0, waiting for transfers between devices: 521 us -> none
    reduce_scatter x8 -> x0, waiting for transfers between devices: 449 us -> none  [the longest x2 123 us: layer_backward(): lax.psum_scatter(up_weight_grad.astype(jnp.bfloat16), 'row', scatter_dime...]
    all_gather x12 -> x0, waiting for transfers between devices: 371 us -> none  [the longest x4 201 us: gather_grads(): return lax.all_gather(rounded, 'col', axis=1, tiled=True)]
    pallas_call x0 -> x18, Pallas kernels: none -> 357 us  [call(): pl.pallas_call(body, out_shape=tuple((shape for shape, _ in outs)), in_sp...]
    psum x8 -> x0, blocking collectives: 175 us -> none  [feature_sums(): return lax.psum((first_sum, second_sum), 'col')]
    all_gather x6 -> x0, blocking collectives: 115 us -> none  [the longest x2 39 us: fetch_layer(): lax.all_gather(joined_part, 'row', axis=0, tiled=True)]
    unnamed x2 -> x0, blocking collectives: 55.7 us -> none
    dot_general x24, matrix products: 79.3 us -> 39.7 us  [the longest x8 15.5 us: dot(): return jnp.dot(left, right, preferred_element_type=jnp.float32)]
  transfers between devices with their start and end apart: 28 -> 0, of which waited for: 26 -> 0; matrix products, arithmetic and copies ran while one was open for 5% -> 0% of each run, Pallas kernels for 0% -> 0%
where the time goes in v1:
time: 560 us; the launch traced here: 549 us
  Pallas kernels  357 us (64%)
  matrix products  71.8 us (13%)
  local copies, waits for them, and re-layouts  68.8 us (12%)
  other arithmetic  34.8 us (6%)
  loops' own time  13.9 us (2%)
    pallas_call x18, Pallas kernels, call(): pl.pallas_call(body, out_shape=tuple((shape for shape, _ in outs)), in_sp...  357 us
    dot_general x8, matrix products, dot(): return jnp.dot(left, right, preferred_element_type=jnp.float32)  15.5 us
    dot_general x8, matrix products, block_scores(): jnp.einsum('qhd,khd->hqk', query_block, key_rows, preferred_element_type=...  14.3 us
    unnamed x211, local copies, waits for them, and re-layouts  14.2 us
    dot_general x8, matrix products, dot_t(): lax.dot_general(left, right, (((1,), (1,)), ((), ())), preferred_element_...  13.2 us

profile of v1, /device:TPU:0, one launch (start us, length us, event | category | flops | bytes accessed | tf_op | source)
XLA Modules:
  0.0 549.5 jit_solution(16112854750112140938)
XLA Ops:
  15.1 33.1 %enter.1 = (f32[128,1024]{1,0:T(8,128)S(1)}, f32[128,1024]{1,0:T(8,128)S(1)}, bf16[1024,512]{1,0:T(8,128)(2,1)S(1)}, f32[8,16,1,256]{3,2,1,0:T(1,128)S(1)}) custom-call(f32[1024,128]{1,0:T(8,128)S(1)} %copy-done.4, f32[1024,128]{1,0:T(8,128)S(1)} %copy-done.5, bf16[64,512]{1,0:T(8,128)(2,1)S(1)} %get-tuple-element.592.weights, f32[1,1,256]{2,1,0:T(1,128)S(1)} %bitcast.317), custom_call_target="tpu_custom_call" | custom-call | tf_op jit(solution)/shard_map/enter/pallas_call | solution.py:540
  59.7 13.7 %gather_rows.3 = bf16[1024,1024]{1,0:T(8,128)(2,1)S(1)} custom-call(bf16[128,1024]{1,0:T(8,128)(2,1)S(1)} %get-tuple-element.540.src), custom_call_target="tpu_custom_call" | custom-call | tf_op jit(solution)/shard_map/gather_rows/pallas_call | solution.py:540
  73.4 20.2 %gather_rows_weights.3 = (bf16[1024,1024]{1,0:T(8,128)(2,1)S(1)}, bf16[1024,512]{1,0:T(8,128)(2,1)S(1)}) custom-call(bf16[128,1024]{1,0:T(8,128)(2,1)S(1)} %get-tuple-element.601.src, bf16[64,512]{1,0:T(8,128)(2,1)S(1)} %copy-done.11), custom_call_target="tpu_custom_call" | custom-call | tf_op jit(solution)/shard_map/gather_rows_weights/pallas_call | solution.py:540
  93.7 2.7 fusion.92
  98.2 15.8 %while.56 = (s32[]{:T(128)}, bf16[2,512,2,64]{1,3,2,0:T(8,128)(2,1)}, f32[2,2,512]{2,1,0:T(2,128)S(1)}, s32[2]{0:T(128)S(1)}, s32[1024]{0:T(1024)S(1)}, /*index=...) while((s32[]{:T(128)}, ...), condition=%wide.region_7.8_spmd.clone, body=%wide.region_4.7_spmd.clone.sunk | while | flops 289996288 | bytes 27051324 | solution.py:835
  117.2 20.7 %spread_rows_weights.2 = (f32[128,1024]{1,0:T(8,128)S(1)}, bf16[1024,512]{1,0:T(8,128)(2,1)S(1)}) custom-call(bf16[1024,1024]{1,0:T(8,128)(2,1)S(1)} %convolution_convert_fusion.7.part, bf16[64,512]{1,0:T(8,128)(2,1)S(1)} %get-tuple-element.588.own), custom_call_target="tpu_custom_call" | custom-call | tf_op jit(solution)/shard_map/spread_rows_weights/pallas_call | solution.py:540
  138.5 21.1 %gather_rows_weights.4 = (bf16[1024,1024]{1,0:T(8,128)(2,1)S(1)}, bf16[1024,512]{1,0:T(8,128)(2,1)S(1)}) custom-call(bf16[128,1024]{1,0:T(8,128)(2,1)S(1)} %add_convert_fusion.2.src, bf16[64,512]{1,0:T(8,128)(2,1)S(1)} %get-tuple-element.591.own), custom_call_target="tpu_custom_call" | custom-call | tf_op jit(solution)/shard_map/gather_rows_weights/pallas_call | solution.py:540
  163.8 20.2 %spread_rows_weights.3 = (f32[128,1024]{1,0:T(8,128)S(1)}, bf16[1024,512]{1,0:T(8,128)(2,1)S(1)}) custom-call(bf16[1024,1024]{1,0:T(8,128)(2,1)S(1)} %convolution_convert_fusion.5.part, bf16[64,512]{1,0:T(8,128)(2,1)S(1)} %get-tuple-element.589.own), custom_call_target="tpu_custom_call" | custom-call | tf_op jit(solution)/shard_map/spread_rows_weights/pallas_call | solution.py:540
  185.1 22.4 %gather_rows_weights.5 = (bf16[1024,1024]{1,0:T(8,128)(2,1)S(1)}, bf16[1024,512]{1,0:T(8,128)(2,1)S(1)}) custom-call(bf16[128,1024]{1,0:T(8,128)(2,1)S(1)} %add_convert_fusion.1.src, bf16[64,512]{1,0:T(8,128)(2,1)S(1)} %get-tuple-element.587.own), custom_call_target="tpu_custom_call" | custom-call | tf_op jit(solution)/shard_map/gather_rows_weights/pallas_call | solution.py:540
  210.8 15.8 %while.57 = (s32[]{:T(128)}, bf16[2,512,2,64]{1,3,2,0:T(8,128)(2,1)}, f32[2,2,512]{2,1,0:T(2,128)S(1)}, s32[2]{0:T(128)S(1)}, s32[1024]{0:T(1024)S(1)}, /*index=...) while((s32[]{:T(128)}, ...), condition=%wide.region_15.16_spmd.clone, body=%wide.region_12.15_spmd.clone.sunk | while | flops 289996288 | bytes 26002720 | solution.py:835
  224.0 1.9 fusion.229
  230.3 12.8 %spread_rows.4 = f32[128,1024]{1,0:T(8,128)S(1)} custom-call(bf16[1024,1024]{1,0:T(8,128)(2,1)S(1)} %convolution_convert_fusion.6.part), custom_call_target="tpu_custom_call" | custom-call | tf_op jit(solution)/shard_map/spread_rows/pallas_call | solution.py:540
  243.7 14.8 %gather_rows.2 = bf16[1024,1024]{1,0:T(8,128)(2,1)S(1)} custom-call(bf16[128,1024]{1,0:T(8,128)(2,1)S(1)} %add_convert_fusion.src), custom_call_target="tpu_custom_call" | custom-call | tf_op jit(solution)/shard_map/gather_rows/pallas_call | solution.py:540
  261.2 2.8 convert_reduce_fusion
  265.5 14.5 %spread_rows.5 = f32[128,1024]{1,0:T(8,128)S(1)} custom-call(bf16[1024,1024]{1,0:T(8,128)(2,1)S(1)} %convolution_convert_fusion.4.part), custom_call_target="tpu_custom_call" | custom-call | tf_op jit(solution)/shard_map/spread_rows/pallas_call | solution.py:540
  282.7 19.4 %spread_rows_grads.2 = (f32[128,1024]{1,0:T(8,128)S(1)}, f32[64,512]{1,0:T(8,128)S(1)}) custom-call(bf16[1024,1024]{1,0:T(8,128)(2,1)S(1)} %convolution_convert_fusion.3.part, bf16[1024,512]{1,0:T(8,128)(2,1)S(1)} %convolution_convert_fusion.11.grads), custom_call_target="tpu_custom_call" | custom-call | tf_op jit(solution)/shard_map/spread_rows_grads/pallas_call | solution.py:540
  304.9 21.2 %gather_rows_grads.3 = (bf16[1024,1024]{1,0:T(8,128)(2,1)S(1)}, f32[64,512]{1,0:T(8,128)S(1)}) custom-call(bf16[128,1024]{1,0:T(8,128)(2,1)S(1)} %get-tuple-element.542.src, bf16[1024,512]{1,0:T(8,128)(2,1)S(1)} %convolution_convert_fusion.10.part), custom_call_target="tpu_custom_call" | custom-call | tf_op jit(solution)/shard_map/gather_rows_grads/pallas_call | solution.py:540
  329.2 23.3 %while.58 = (s32[]{:T(128)}, f32[1024,2,64]{0,2,1:T(8,128)}, f32[1024,2,64]{0,2,1:T(8,128)}, bf16[2,512,2,64]{1,3,2,0:T(8,128)(2,1)}, s32[2]{0:T(128)S(1)}, /*in...) while((s32[]{:T(128)}, f32[1024,2,64]{0,2,1:T(8,128)}, ...), condition=%wide.region_22.23_spmd.clone, body=%wide.region_20.22_spmd.clone.sunk | while | flops 685964800 | bytes 50893788 | solution.py:884
  334.0 2.1 multiply_reduce_fusion.20
  345.7 2.1 multiply_reduce_fusion.20
  364.1 14.5 %spread_rows.6 = f32[128,1024]{1,0:T(8,128)S(1)} custom-call(bf16[1024,1024]{1,0:T(8,128)(2,1)S(1)} %convolution_convert_fusion.1.part), custom_call_target="tpu_custom_call" | custom-call | tf_op jit(solution)/shard_map/spread_rows/pallas_call | solution.py:540
  381.0 19.2 %gather_rows_grads.4 = (bf16[1024,1024]{1,0:T(8,128)(2,1)S(1)}, f32[64,512]{1,0:T(8,128)S(1)}) custom-call(bf16[128,1024]{1,0:T(8,128)(2,1)S(1)} %get-tuple-element.534.src, bf16[1024,512]{1,0:T(8,128)(2,1)S(1)} %pad_maximum_fusion.part), custom_call_target="tpu_custom_call" | custom-call | tf_op jit(solution)/shard_map/gather_rows_grads/pallas_call | solution.py:540
  400.2 4.1 convert_reduce_fusion.1
  408.7 2.8 convolution_convert_fusion.2.part
  411.6 20.9 %spread_rows_grads.3 = (f32[128,1024]{1,0:T(8,128)S(1)}, f32[64,512]{1,0:T(8,128)S(1)}) custom-call(bf16[1024,1024]{1,0:T(8,128)(2,1)S(1)} %convolution_convert_fusion.2.part, bf16[1024,512]{1,0:T(8,128)(2,1)S(1)} %convolution_convert_fusion.9.grads), custom_call_target="tpu_custom_call" | custom-call | tf_op jit(solution)/shard_map/spread_rows_grads/pallas_call | solution.py:540
  436.6 22.0 %gather_rows_grads.5 = (bf16[1024,1024]{1,0:T(8,128)(2,1)S(1)}, f32[64,512]{1,0:T(8,128)S(1)}) custom-call(bf16[128,1024]{1,0:T(8,128)(2,1)S(1)} %get-tuple-element.537.src, bf16[1024,512]{1,0:T(8,128)(2,1)S(1)} %convolution_convert_fusion.8.part), custom_call_target="tpu_custom_call" | custom-call | tf_op jit(solution)/shard_map/gather_rows_grads/pallas_call | solution.py:540
  463.2 19.9 %while.59 = (s32[]{:T(128)}, f32[1024,2,64]{0,2,1:T(8,128)S(1)}, f32[1024,2,64]{0,2,1:T(8,128)S(1)}, bf16[2,512,2,64]{1,3,2,0:T(8,128)(2,1)}, s32[2]{0:T(128)S(1...) while((s32[]{:T(128)}, f32[1024,2,64]{0,2,1:T(8,128)S(1)}, ...), condition=%wide.region_29.30_spmd.clone, body=%wide.region_27.29_spmd.clone.sunk | while | flops 685964800 | bytes 43553672 | solution.py:884
  468.4 2.1 multiply_reduce_fusion.21
  478.2 2.1 multiply_reduce_fusion.21
  491.8 14.5 %spread_rows.7 = f32[128,1024]{1,0:T(8,128)S(1)} custom-call(bf16[1024,1024]{1,0:T(8,128)(2,1)S(1)} %convolution_convert_fusion.part), custom_call_target="tpu_custom_call" | custom-call | tf_op jit(solution)/shard_map/spread_rows/pallas_call | solution.py:540
  511.0 31.9 %leave.1 = (f32[1024,128]{1,0:T(8,128)S(1)}, f32[1024,128]{1,0:T(8,128)S(1)}, f32[64,512]{1,0:T(8,128)S(1)}, f32[1,1,256]{2,1,0:T(1,128)S(1)}) custom-call(f32[128,1024]{1,0:T(8,128)S(1)} %get-tuple-element.570.hid, f32[128,1024]{1,0:T(8,128)S(1)} %multiply_add_fusion.4.cot, bf16[1024,512]{1,0:T(8,128)(2,1)S(1)} %pad_maximum_fusion.1.grads, ...), custom_call_target="tpu_custom_call" | custom-call | tf_op jit(solution)/shard_map/leave/pallas_call | solution.py:540
  546.4 1.9 copy.272
  (579 shorter events, 150.9 us)
Async XLA Ops:
  49.3 88.7 %copy-start = (f32[128,1024]{1,0:T(8,128)}, f32[128,1024]{1,0:T(8,128)S(1)}, u32[]{:S(2)}) copy-start(f32[128,1024]{1,0:T(8,128)S(1)} %get-tuple-element.267) | copy-start | bytes 1572868
  51.4 110.8 %copy-start.99 = (f32[512]{0:T(512)}, f32[512]{0:T(512)S(1)}, u32[]{:S(2)}) copy-start(f32[512]{0:T(512)S(1)} %dynamic_slice.74) | copy-start | bytes 6148
  56.3 128.0 %copy-start.78 = (f32[1024]{0:T(1024)}, f32[1024]{0:T(1024)S(1)}, u32[]{:S(2)}) copy-start(f32[1024]{0:T(1024)S(1)} %mul.474) | copy-start | bytes 12292
  57.5 80.9 %copy-start.76 = (f32[1024]{0:T(1024)}, f32[1024]{0:T(1024)S(1)}, u32[]{:S(2)}) copy-start(f32[1024]{0:T(1024)S(1)} %mul.461) | copy-start | bytes 12292
  58.7 34.9 %copy-start.74 = (f32[1024]{0:T(1024)}, f32[1024]{0:T(1024)S(1)}, u32[]{:S(2)}) copy-start(f32[1024]{0:T(1024)S(1)} %mul.452) | copy-start | bytes 12292
  114.0 23.9 %copy-start.25 = (bf16[1024,2,64]{0,2,1:T(8,128)(2,1)}, bf16[1024,2,64]{0,2,1:T(8,128)(2,1)S(1)}, u32[]{:S(2)}) copy-start(bf16[1024,2,64]{0,2,1:T(8,128)(2,1)S(1)} %get-tuple-element.1084) | copy-start | bytes 786436
  114.0 23.9 %copy-start.27 = (bf16[1024,2,64]{0,2,1:T(8,128)(2,1)}, bf16[1024,2,64]{0,2,1:T(8,128)(2,1)S(1)}, u32[]{:S(2)}) copy-start(bf16[1024,2,64]{0,2,1:T(8,128)(2,1)S(1)} %get-tuple-element.1086) | copy-start | bytes 786436
  114.0 23.9 %copy-start.72 = (f32[2,2,512]{2,1,0:T(2,128)}, f32[2,2,512]{2,1,0:T(2,128)S(1)}, u32[]{:S(2)}) copy-start(f32[2,2,512]{2,1,0:T(2,128)S(1)} %get-tuple-element.1011) | copy-start | bytes 24580
  115.4 22.5 %copy-start.44 = (bf16[16,8,2,512]{3,1,2,0:T(8,128)(2,1)}, bf16[16,8,2,512]{3,1,2,0:T(8,128)(2,1)S(1)}, u32[]{:S(2)}) copy-start(bf16[16,8,2,512]{3,1,2,0:T(8,128)(2,1)S(1)} %copy.171) | copy-start | bytes 786436
  137.9 24.3 %copy-start.20 = (bf16[1024,512]{1,0:T(8,128)(2,1)}, bf16[1024,512]{1,0:T(8,128)(2,1)S(1)}, u32[]{:S(2)}) copy-start(bf16[1024,512]{1,0:T(8,128)(2,1)S(1)} %get-tuple-element.275) | copy-start | bytes 3145732
  137.9 23.0 %copy-start.19 = (bf16[1024,512]{1,0:T(8,128)(2,1)S(1)}, bf16[1024,512]{1,0:T(8,128)(2,1)}, u32[]{:S(2)}) copy-start(bf16[1024,512]{1,0:T(8,128)(2,1)} %copy-done.18) | copy-start | bytes 3145732
  138.1 45.8 %copy-start.33 = (f32[128,1024]{1,0:T(8,128)}, f32[128,1024]{1,0:T(8,128)S(1)}, u32[]{:S(2)}) copy-start(f32[128,1024]{1,0:T(8,128)S(1)} %get-tuple-element.553) | copy-start | bytes 1572868
  138.1 24.1 %copy-start.88 = (f32[128]{0:T(128)}, f32[128]{0:T(128)S(1)}, u32[]{:S(2)}) copy-start(f32[128]{0:T(128)S(1)} %broadcast_multiply_fusion.10) | copy-start | bytes 1540
  138.4 23.9 %copy-start.94 = (f32[128]{0:T(128)}, f32[128]{0:T(128)S(1)}, u32[]{:S(2)}) copy-start(f32[128]{0:T(128)S(1)} %add_rsqrt_fusion.2) | copy-start | bytes 1540
  159.6 47.9 %copy-start.9 = (bf16[1024,512]{1,0:T(8,128)(2,1)}, bf16[1024,512]{1,0:T(8,128)(2,1)S(1)}, u32[]{:S(2)}) copy-start(bf16[1024,512]{1,0:T(8,128)(2,1)S(1)} %get-tuple-element.278) | copy-start | bytes 3145732
  163.7 20.2 %copy-start.85 = (f32[1024]{0:T(1024)S(1)}, f32[1024]{0:T(1024)}, u32[]{:S(2)}) copy-start(f32[1024]{0:T(1024)} %add.410) | copy-start | bytes 12292
  163.7 21.2 %copy-start.84 = (f32[1024]{0:T(1024)S(1)}, f32[1024]{0:T(1024)}, u32[]{:S(2)}) copy-start(f32[1024]{0:T(1024)} %add.414) | copy-start | bytes 12292
  184.1 24.5 %copy-start.35 = (f32[128,1024]{1,0:T(8,128)}, f32[128,1024]{1,0:T(8,128)S(1)}, u32[]{:S(2)}) copy-start(f32[128,1024]{1,0:T(8,128)S(1)} %get-tuple-element.551) | copy-start | bytes 1572868
  184.1 24.5 %copy-start.90 = (f32[128]{0:T(128)}, f32[128]{0:T(128)S(1)}, u32[]{:S(2)}) copy-start(f32[128]{0:T(128)S(1)} %broadcast_multiply_fusion.9) | copy-start | bytes 1540
  185.0 23.7 %copy-start.96 = (f32[128]{0:T(128)}, f32[128]{0:T(128)S(1)}, u32[]{:S(2)}) copy-start(f32[128]{0:T(128)S(1)} %add_rsqrt_fusion.1) | copy-start | bytes 1540
  282.6 19.7 %copy-start.3 = (f32[128,1024]{1,0:T(8,128)S(1)}, f32[128,1024]{1,0:T(8,128)}, u32[]{:S(2)}) copy-start(f32[128,1024]{1,0:T(8,128)} %copy-done.2) | copy-start | bytes 1572868
  282.7 19.7 %copy-start.82 = (f32[1024]{0:T(1024)S(1)}, f32[1024]{0:T(1024)}, u32[]{:S(2)}) copy-start(f32[1024]{0:T(1024)} %add.436) | copy-start | bytes 12292
  302.4 23.7 %copy-start.47 = (bf16[16,8,2,512]{3,1,2,0:T(8,128)(2,1)S(1)}, bf16[16,8,2,512]{3,1,2,0:T(8,128)(2,1)}, u32[]{:S(2)}) copy-start(bf16[16,8,2,512]{3,1,2,0:T(8,128)(2,1)} %copy-done.46) | copy-start | bytes 786436
  379.9 20.3 %copy-start.100 = (f32[512]{0:T(512)S(1)}, f32[512]{0:T(512)}, u32[]{:S(2)}) copy-start(f32[512]{0:T(512)} %copy-done.99) | copy-start | bytes 6148
  380.8 19.4 %copy-start.108 = (f32[1024,512]{1,0:T(8,128)S(1)}, f32[1024,512]{1,0:T(8,128)}, u32[]{:S(2)}) copy-start(f32[1024,512]{1,0:T(8,128)} %copy-done.107) | copy-start | bytes 6291460
  381.0 23.3 %copy-start.61 = (f32[1,8,8,16,8]{4,3,2,1,0:T(8,128)}, f32[1,8,8,16,8]{4,3,2,1,0:T(8,128)S(1)}, u32[]{:S(2)}) copy-start(f32[1,8,8,16,8]{4,3,2,1,0:T(8,128)S(1)} %constant_dynamic-update-slice_fusion.8) | copy-start | bytes 98308
  411.5 21.7 %copy-start.34 = (f32[128,1024]{1,0:T(8,128)S(1)}, f32[128,1024]{1,0:T(8,128)}, u32[]{:S(2)}) copy-start(f32[128,1024]{1,0:T(8,128)} %copy-done.33) | copy-start | bytes 1572868
  411.5 21.7 %copy-start.77 = (f32[1024]{0:T(1024)S(1)}, f32[1024]{0:T(1024)}, u32[]{:S(2)}) copy-start(f32[1024]{0:T(1024)} %copy-done.76) | copy-start | bytes 12292
  411.5 21.7 %copy-start.89 = (f32[128]{0:T(128)S(1)}, f32[128]{0:T(128)}, u32[]{:S(2)}) copy-start(f32[128]{0:T(128)} %copy-done.88) | copy-start | bytes 1540
  411.5 21.7 %copy-start.95 = (f32[128]{0:T(128)S(1)}, f32[128]{0:T(128)}, u32[]{:S(2)}) copy-start(f32[128]{0:T(128)} %copy-done.94) | copy-start | bytes 1540
  411.6 21.9 %copy-start.54 = (f32[128,1024]{1,0:T(8,128)S(1)}, f32[128,1024]{1,0:T(8,128)}, u32[]{:S(2)}) copy-start(f32[128,1024]{1,0:T(8,128)} %get-tuple-element.535) | copy-start | bytes 1572868
  433.5 25.9 %copy-start.45 = (bf16[16,8,2,512]{3,1,2,0:T(8,128)(2,1)S(1)}, bf16[16,8,2,512]{3,1,2,0:T(8,128)(2,1)}, u32[]{:S(2)}) copy-start(bf16[16,8,2,512]{3,1,2,0:T(8,128)(2,1)} %copy-done.44) | copy-start | bytes 786436
  (92 other events, 347.3 us)
